TPU v7x, 256 devices: a whole 4x4x8 slice. The times are simulated.
256 devices in a mesh: pool: 64 (over z, x, core), blk: 4 (over y).
Axes of the slice: x: 4, y: 4, z: 8, core: 2. Of those that a mesh axis runs over, the one named last changes fastest.
Arguments:
- query_emb: bfloat16 [65536, 512], P(('pool', 'blk')), may hold values from -5.4 to 5.4
- item_table: bfloat16 [131072, 1024], P(('pool', 'blk')), may hold values from -24 to 24
- w_in: bfloat16 [1024, 3072], replicated, may hold values from -0.1875 to 0.1875
- bias_in: float32 [3072], replicated, may hold values from -3 to 3
- w_out: bfloat16 [3072, 512], replicated, may hold values from -0.109375 to 0.109375
- fetch_rows: int32 [16384, 16], P(('pool', 'blk')), may hold values from 0 to 511, as said below
- fetch_counts: int32 [256, 64], P(('pool', 'blk')), may hold values from 0 to 16, as said below
- pos_slot: int32 [65536], P(('pool', 'blk')), may hold values from 0 to 511
Outputs:
- query_loss: float32 [65536], P(('pool', 'blk'))
- query_grad: float32 [65536, 512], P(('pool', 'blk'))
- table_grad: float32 [131072, 1024], P(('pool', 'blk'))
Inputs may be any that keep to these rules, and one draw needn't show every extreme that they name: `fetch_rows`: the first fetch_counts[d, o] slots of a row name distinct rows of the shard; later slots are in range and ask for nothing. `fetch_counts`: each device's counts sum to exactly 512. In every draw each blk slice has one shard to which every device of the slice sends exactly 16 rows. `pos_slot`: several queries of a device may share one positive.
All inputs are finite; a program needn't handle non-finite values.
Results may differ from a plain program's by a relative error of at most 0.01825.
Values may be sent and summed in bfloat16 or wider, within the bound.
A program may use at most 128 MiB of HBM per device.

v0:
```python
import jax
import jax.numpy as jnp
from jax import lax
from jax.sharding import PartitionSpec as P

ROWS_DEV = 512


logit_scale = 80.0
norm_eps = 1e-06


def live_order(counts, live_total, capacity):
    count_ends = jnp.cumsum(counts)
    count_starts = count_ends - counts
    position = jnp.arange(live_total, dtype=jnp.int32)
    owner_of = jnp.sum((count_ends[None, :] <= position[:, None]).astype(jnp.int32), axis=1)
    within_slot = position - jnp.take(count_starts, owner_of)
    slot_of = owner_of * capacity + within_slot
    slot_column = jnp.arange(capacity, dtype=jnp.int32)
    inverse = jnp.where(
        slot_column[None, :] < counts[:, None],
        count_starts[:, None] + slot_column[None, :],
        live_total,
    )
    return (slot_of, inverse.reshape(-1))


def on_device(query_emb, item_table, w_in, bias_in, w_out, fetch_rows, fetch_counts, pos_slot):
    owners = lax.axis_size("pool")
    capacity = fetch_rows.shape[1]
    feat_dim = item_table.shape[1]
    rows_here = ROWS_DEV
    own_index = lax.axis_index("blk")
    slot_of, inverse = live_order(fetch_counts[0], rows_here, capacity)
    asked_rows = lax.all_to_all(fetch_rows, "pool", split_axis=0, concat_axis=0, tiled=True)
    served = jnp.take(item_table, asked_rows.reshape(-1), axis=0).reshape(
        owners, capacity, feat_dim
    )
    arrived = lax.all_to_all(served, "pool", split_axis=0, concat_axis=0, tiled=True)
    features = jnp.take(arrived.reshape(owners * capacity, feat_dim), slot_of, axis=0)
    pre_act = jnp.dot(features, w_in, preferred_element_type=jnp.float32) + bias_in
    hidden = jax.nn.silu(pre_act).astype(jnp.bfloat16)
    tower_out = jnp.dot(hidden, w_out, preferred_element_type=jnp.float32)
    item_inv = lax.rsqrt(jnp.sum(tower_out * tower_out, axis=1, keepdims=True) + norm_eps)
    item_vec = (tower_out * item_inv).astype(jnp.bfloat16)
    query_f = query_emb.astype(jnp.float32)
    query_inv = lax.rsqrt(jnp.sum(query_f * query_f, axis=1, keepdims=True) + norm_eps)
    query_vec = (query_f * query_inv).astype(jnp.bfloat16)
    blocks = lax.all_gather(item_vec, "blk", axis=0, tiled=True)
    scores = logit_scale * lax.dot_general(
        query_vec, blocks, (((1,), (1,)), ((), ())), preferred_element_type=jnp.float32
    )
    totals = jnp.log(jnp.sum(jnp.exp(scores), axis=1))
    target = own_index * rows_here + pos_slot
    picked = jnp.take_along_axis(scores, target[:, None], axis=1)[:, 0]
    query_loss = totals - picked
    columns = jnp.arange(scores.shape[1], dtype=jnp.int32)
    target_hit = (columns[None, :] == target[:, None]).astype(jnp.float32)
    grad_coef = (jnp.exp(scores - totals[:, None]) - target_hit).astype(jnp.bfloat16)
    vec_grad = logit_scale * jnp.dot(grad_coef, blocks, preferred_element_type=jnp.float32)
    query_grad = vec_grad * query_inv - query_f * query_inv**3 * jnp.sum(
        query_f * vec_grad, axis=1, keepdims=True
    )
    item_grad = lax.psum_scatter(
        (
            logit_scale
            * lax.dot_general(
                grad_coef, query_vec, (((0,), (0,)), ((), ())), preferred_element_type=jnp.float32
            )
        ).astype(jnp.bfloat16),
        "blk",
        scatter_dimension=0,
        tiled=True,
    ).astype(jnp.float32)
    tower_grad = (
        item_grad * item_inv
        - tower_out * item_inv**3 * jnp.sum(tower_out * item_grad, axis=1, keepdims=True)
    ).astype(jnp.bfloat16)
    hidden_grad = lax.dot_general(
        tower_grad, w_out, (((1,), (1,)), ((), ())), preferred_element_type=jnp.float32
    )
    gate_sig = jax.nn.sigmoid(pre_act)
    pre_grad = (hidden_grad * gate_sig * (1.0 + pre_act * (1.0 - gate_sig))).astype(jnp.bfloat16)
    feats_grad = lax.dot_general(
        pre_grad, w_in, (((1,), (1,)), ((), ())), preferred_element_type=jnp.float32
    )
    padded = jnp.concatenate([feats_grad, jnp.zeros((1, feat_dim), jnp.float32)], axis=0)
    slot_grads = jnp.take(padded, inverse, axis=0).reshape(owners, capacity, feat_dim)
    returned = lax.all_to_all(
        slot_grads.astype(jnp.bfloat16), "pool", split_axis=0, concat_axis=0, tiled=True
    ).astype(slot_grads.dtype)
    table_grad = jax.ops.segment_sum(
        returned.reshape(owners * capacity, feat_dim),
        asked_rows.reshape(-1),
        num_segments=item_table.shape[0],
    )
    return (query_loss, query_grad, table_grad)


def solution(mesh):
    placed = (
        P(("pool", "blk"), None),
        P(("pool", "blk"), None),
        P(),
        P(),
        P(),
        P(("pool", "blk"), None),
        P(("pool", "blk"), None),
        P(("pool", "blk")),
    )
    return jax.shard_map(
        on_device,
        mesh=mesh,
        in_specs=placed,
        out_specs=(P(("pool", "blk")), P(("pool", "blk"), None), P(("pool", "blk"), None)),
        check_vma=False,
    )
```

profile of v0, /device:TPU:1, one launch (start us, length us, event | category | flops | bytes accessed | tf_op | source)
XLA Modules:
  0.0 294.5 jit_solution(11014182456502219195)
XLA Ops:
  7.2 0.9 copy.26
  8.1 22.3 %all_to_all.19 = s32[64,1,16]{2,1,0:T(1,128)S(1)} all-to-all(s32[64,1,16]{2,1,0:T(1,128)S(1)} %bitcast.96), channel_id=1, replica_groups=mesh['pool'=64,'blk'=4] {'pool'}, dimensions={0} | all-to-all | bytes 8192 | tf_op jit(solution)/shard_map/all_to_all | solution.py:36
  30.4 0.5 broadcast.710
  30.9 0.7 reduce.120
  31.7 0.1 reshape.289
  31.8 7.4 %gather_fusion = bf16[1024,1024]{1,0:T(8,128)(2,1)} fusion(bf16[512,1024]{1,0:T(8,128)(2,1)} %param.9, s32[1024]{0:T(1024)S(1)} %broadcast_clamp_fusion.1), kind=kCustom, calls=%fused_computation | custom fusion | bytes 4198400 | tf_op jit(solution)/shard_map/jit(_take)/gather | solution.py:37
  39.1 3.2 %broadcast_select_fusion = bf16[64,16,1024]{2,1,0:T(8,128)(2,1)} fusion(bf16[64,16,1024]{2,1,0:T(8,128)(2,1)} %bitcast.93, pred[64,16]{1,0:T(8,128)(4,1)S(1)} %compare_and_fusion.1), kind=kLoop, calls=%fused_computation.18 | loop fusion | flops 1048576 | bytes 4195328 | tf_op jit(solution)/shard_map/jit(_take)/select_n | solution.py:37
  42.3 5.7 %all-to-all-start.1 = ((bf16[64,16,1024]{2,1,0:T(8,128)(2,1)}), bf16[64,16,1024]{2,1,0:T(8,128)(2,1)}, u32[]{:S(2)}, u32[]{:S(2)}) async-start(bf16[64,16,1024]{2,1,0:T(8,128)(2,1)} %broadcast_select_fusion), calls=%async_computation.1 | async-start | bytes 4194304 | tf_op jit(solution)/shard_map/all_to_all | solution.py:40
  48.1 0.1 copy.25
  48.2 0.1 reduce-window.7
  48.3 0.1 reduce
  48.4 0.7 fusion.40
  49.1 0.7 fusion.39
  49.8 0.7 fusion.38
  50.5 0.7 fusion.37
  51.3 0.1 convert_reduce_fusion
  51.4 4.3 %compare_select_fusion.6 = (s32[512,1]{0,1:T(1,128)S(1)}, s32[512,1]{0,1:T(1,128)S(1)}) fusion(s32[]{:T(128)} %bitcast.60, s32[]{:T(128)} %bitcast.61, s32[]{:T(128)} %bitcast.62, s32[]{:T(128)} %bitcast.63, s32[]{:T(128)} %bitcast.64, s32[]{:T(128)} %bitcast.66, s32[]{:T(128)} %bitcast.65, s32[512,1]{0,1:T(1,128)S(1)} %bitcast.97), kind=kLoop, calls=%fused_computation.112 | loop fusion | flops 7680 | bytes 6172 | tf_op jit(solution)/shard_map/jit(_take)/gather | solution.py:18
  55.7 0.4 compare_reduce_fusion.56
  56.1 35.6 %compare_and_fusion.2 = (pred[512]{0:T(512)(128)(4,1)S(1)}, s32[512]{0:T(512)S(1)}) fusion(s32[512]{0:T(512)S(1)} %convert_reduce_fusion, pred[512]{0:T(512)(128)(4,1)S(1)} %get-tuple-element.59, pred[512]{0:T(512)(128)(4,1)S(1)} %get-tuple-element.57, pred[512]{0:T(512)(128)(4,1)S(1)} %get-tuple-element.58, pred[512]{0:T(512)(128)(4,1)S(1)} %get-tuple-element.56, ...), kind=kLoop, calls=%fused_computation.131 | loop fusion | flops 37376 | bytes 36068 | tf_op jit(solution)/shard_map/jit(_take)/and | solution.py:41
  91.7 5.9 %all-to-all-done.1 = bf16[64,16,1024]{2,1,0:T(8,128)(2,1)} async-done(((bf16[64,16,1024]{2,1,0:T(8,128)(2,1)}), bf16[64,16,1024]{2,1,0:T(8,128)(2,1)}, u32[]{:S(2)}, u32[]{:S(2)}) %all-to-all-start.1) | async-done | bytes 2097184 | tf_op jit(solution)/shard_map/all_to_all | solution.py:40
  97.7 5.3 %gather_fusion.1 = bf16[512,1024]{1,0:T(8,128)(2,1)} fusion(bf16[1024,1024]{1,0:T(8,128)(2,1)} %bitcast.72, s32[1024]{0:T(1024)S(1)} %pad_clamp_fusion), kind=kCustom, calls=%fused_computation.1 | custom fusion | bytes 2099200 | tf_op jit(solution)/shard_map/jit(_take)/gather | solution.py:41
  103.0 5.9 %fusion.8 = f32[512,3072]{1,0:T(8,128)S(1)} fusion(bf16[1024,3072]{1,0:T(8,128)(2,1)} %param.10, bf16[512,1024]{1,0:T(8,128)(2,1)} %gather_fusion.1, pred[512]{0:T(512)(128)(4,1)S(1)} %get-tuple-element.62), kind=kOutput, calls=%fused_computation.27 | convolution fusion | flops 3221749760 | bytes 13632000 | tf_op jit(solution)/shard_map/dot_general | solution.py:42
  109.0 2.5 multiply_reduce_fusion
  111.4 0.2 copy-done.6
  111.6 1.0 copy-done.1
  112.6 0.9 multiply_convert_fusion.4
  113.5 0.2 reduce-scatter.2.cloned.1.call-start
  113.8 0.1 fusion.11
  114.0 31.0 %all-gather.2.cloned.1.call-done = bf16[2048,512]{0,1:T(8,128)(2,1)} async-done(((bf16[512,512]{0,1:T(8,128)(2,1)}), bf16[2048,512]{0,1:T(8,128)(2,1)}) %all-gather.2.cloned.1.call-update) | async-done | bytes 2097168 | tf_op jit(solution)/shard_map/all_gather | solution.py:50
  145.0 3.7 %exponential_reduce_fusion = (f32[256]{0:T(256)S(1)}, f32[256,2048]{1,0:T(8,128)}) fusion(bf16[2048,512]{0,1:T(8,128)(2,1)} %all-gather.2.cloned.1.call-done, bf16[256,512]{1,0:T(8,128)(2,1)S(1)} %copy-done.2, f32[256]{0:T(256)S(1)} %get-tuple-element.70), kind=kOutput, calls=%fused_computation.17 | convolution fusion | flops 538312448 | bytes 4458496 | tf_op jit(solution)/shard_map/dot_general | solution.py:51
  148.7 3.7 %gather_fusion.3 = f32[256]{0:T(256)S(1)} fusion(f32[256,2048]{1,0:T(8,128)} %get-tuple-element.140, s32[256]{0:T(256)S(1)} %bitcast.91), kind=kCustom, calls=%fused_computation.3 | custom fusion | bytes 4096 | tf_op jit(solution)/shard_map/jit(take_along_axis)/gather | solution.py:56
  152.5 0.6 fusion.36
  153.0 4.0 %multiply_convert_fusion.2 = bf16[2048,512]{0,1:T(8,128)(2,1)} fusion(bf16[256,512]{1,0:T(8,128)(2,1)S(1)} %copy-done.2, f32[256]{0:T(256)S(1)} %get-tuple-element.70, f32[256,2048]{1,0:T(8,128)} %get-tuple-element.140, s32[256]{0:T(256)S(1)} %get-tuple-element.61, f32[256]{0:T(256)S(1)} %get-tuple-element.71), kind=kOutput, calls=%fused_computation.11 | convolution fusion | flops 541982720 | bytes 4459520 | tf_op jit(solution)/shard_map/dot_general | solution.py:68
  157.1 0.1 add_select_fusion
  157.2 0.1 select_n.143
  157.3 0.1 compare_and_fusion
  157.4 32.2 %reduce-scatter.2.cloned.1.call-done = bf16[512,512]{0,1:T(8,128)(2,1)} async-done(((bf16[2048,512]{0,1:T(8,128)(2,1)}), bf16[512,512]{0,1:T(8,128)(2,1)}) %reduce-scatter.2.cloned.1.call-update) | async-done | bytes 524304 | tf_op jit(solution)/shard_map/reduce_scatter | solution.py:65
  189.6 1.5 fusion.6
  191.1 12.0 %fusion.3 = bf16[512,1024]{1,0:T(8,128)(2,1)} fusion(bf16[1024,3072]{1,0:T(8,128)(2,1)} %param.10, f32[512,3072]{1,0:T(8,128)} %copy-done.6, bf16[3072,512]{1,0:T(8,128)(2,1)S(1)} %copy-done, f32[3072]{0:T(1024)S(1)} %copy-done.5, bf16[512,512]{0,1:T(8,128)(2,1)} %reduce-scatter.2.cloned.1.call-done, f32[512,512]{0,1:T(8,128)} %copy-done.1, ...), kind=kOutput, calls=%fused_computation.14 | convolution fusion | flops 4849139712 | bytes 18368512 | tf_op jit(solution)/shard_map/dot_general | solution.py:85
  203.1 2.3 concatenate.3
  205.4 7.4 %gather_fusion.2 = bf16[1024,1024]{1,0:T(8,128)(2,1)} fusion(bf16[513,1024]{1,0:T(8,128)(2,1)} %concatenate.3, s32[1024]{0:T(1024)S(1)} %broadcast_clamp_fusion), kind=kCustom, calls=%fused_computation.2 | custom fusion | bytes 4198400 | tf_op jit(solution)/shard_map/jit(_take)/gather | solution.py:89
  212.8 3.4 %select_convert_fusion = bf16[64,16,1024]{2,1,0:T(8,128)(2,1)} fusion(bf16[64,16,1024]{2,1,0:T(8,128)(2,1)} %bitcast.92, pred[64,16]{1,0:T(8,128)(4,1)S(1)} %compare_and_fusion), kind=kLoop, calls=%fused_computation.10 | loop fusion | flops 1048576 | bytes 4195328 | tf_op jit(solution)/shard_map/convert_element_type | solution.py:91
  216.2 10.8 %all-to-all-start.2 = ((bf16[64,16,1024]{2,1,0:T(8,128)(2,1)}), bf16[64,16,1024]{2,1,0:T(8,128)(2,1)}, u32[]{:S(2)}, u32[]{:S(2)}) async-start(bf16[64,16,1024]{2,1,0:T(8,128)(2,1)} %select_convert_fusion), calls=%async_computation.3 | async-start | bytes 4194304 | tf_op jit(solution)/shard_map/all_to_all | solution.py:90
  227.0 0.1 reshape.401
  227.1 3.1 %fusion.15 = (f32[256]{0:T(256)S(1)}, f32[256,512]{1,0:T(8,128)S(1)}) fusion(bf16[256,512]{1,0:T(8,128)(2,1)S(1)} %copy-done.2, bf16[2048,512]{0,1:T(8,128)(2,1)} %all-gather.2.cloned.1.call-done, f32[256,2048]{1,0:T(8,128)} %get-tuple-element.140, s32[256]{0:T(256)S(1)} %get-tuple-element.61, f32[256]{0:T(256)S(1)} %get-tuple-element.71), kind=kOutput, calls=%fused_computation.38 | convolution fusion | flops 540016384 | bytes 4983808 | tf_op jit(solution)/shard_map/dot_general | solution.py:61
  230.2 1.0 fusion.14
  231.1 45.4 %all-to-all-done.2 = bf16[64,16,1024]{2,1,0:T(8,128)(2,1)} async-done(((bf16[64,16,1024]{2,1,0:T(8,128)(2,1)}), bf16[64,16,1024]{2,1,0:T(8,128)(2,1)}, u32[]{:S(2)}, u32[]{:S(2)}) %all-to-all-start.2) | async-done | bytes 2097184 | tf_op jit(solution)/shard_map/all_to_all | solution.py:90
  276.6 11.1 %scatter_custom_fusion = f32[512,1024]{1,0:T(8,128)} fusion(s32[1024]{0:T(1024)S(1)} %reshape.401, bf16[1024,1024]{1,0:T(8,128)(2,1)} %bitcast.81, f32[]{:T(128)} %constant.54.clone.1), kind=kCustom, calls=%fused_computation.8 | custom fusion | flops 2097152 | bytes 4194308 | tf_op jit(solution)/shard_map/scatter-add | solution.py:93
  (29 shorter events, 0.2 us)
Async XLA Ops:
  7.2 101.8 %copy-start = (bf16[3072,512]{1,0:T(8,128)(2,1)S(1)}, bf16[3072,512]{1,0:T(8,128)(2,1)}, u32[]{:S(2)}) copy-start(bf16[3072,512]{1,0:T(8,128)(2,1)} %param.12) | copy-start | bytes 9437188
  42.3 5.8 %copy-start.3 = (s32[1,64]{1,0:T(1,128)S(1)}, s32[1,64]{1,0:T(1,128)}, u32[]{:S(2)}) copy-start(s32[1,64]{1,0:T(1,128)} %param.14) | copy-start | bytes 772
  42.3 55.4 %all-to-all-start.1 = ((bf16[64,16,1024]{2,1,0:T(8,128)(2,1)}), bf16[64,16,1024]{2,1,0:T(8,128)(2,1)}, u32[]{:S(2)}, u32[]{:S(2)}) async-start(bf16[64,16,1024]{2,1,0:T(8,128)(2,1)} %broadcast_select_fusion), calls=%async_computation.1 | async-start | bytes 4194304 | tf_op jit(solution)/shard_map/all_to_all | solution.py:40
  48.1 97.0 %all-gather.2.cloned.1.call-start = ((), (), s32[]{:S(2)}) async-start(), calls=%async_computation.4 | async-start | bytes 2621440 | tf_op jit(solution)/shard_map/all_gather | solution.py:50
  103.0 5.9 %copy-start.5 = (f32[3072]{0:T(1024)S(1)}, f32[3072]{0:T(1024)}, u32[]{:S(2)}) copy-start(f32[3072]{0:T(1024)} %param.11) | copy-start | bytes 36868
  108.9 2.7 copy-start.6
  111.6 1.0 copy-start.1
  111.6 2.2 copy-start.4
  111.6 2.2 copy-start.2
  113.5 76.0 %reduce-scatter.2.cloned.1.call-start = ((), (), s32[]{:S(2)}) async-start(), calls=%async_computation.5 | async-start | bytes 2621440 | tf_op jit(solution)/shard_map/reduce_scatter | solution.py:65
  216.2 60.4 %all-to-all-start.2 = ((bf16[64,16,1024]{2,1,0:T(8,128)(2,1)}), bf16[64,16,1024]{2,1,0:T(8,128)(2,1)}, u32[]{:S(2)}, u32[]{:S(2)}) async-start(bf16[64,16,1024]{2,1,0:T(8,128)(2,1)} %select_convert_fusion), calls=%async_computation.3 | async-start | bytes 4194304 | tf_op jit(solution)/shard_map/all_to_all | solution.py:90
Sparse Core Ops, SparseCore 0:
  113.6 31.3 all-gather.1
  157.2 32.3 reduce-scatter.1
where the time goes:
time: 296 us; the launch traced here: 294 us
  waiting for transfers between devices  115 us (39%)
  other arithmetic  63.3 us (21%)
  local copies, waits for them, and re-layouts  31.9 us (11%)
  matrix products  31.2 us (11%)
  blocking collectives  22.3 us (8%)
  starting transfers between devices  16.8 us (6%)
  between operations  14.3 us (5%)
    all_to_all x1, waiting for transfers between devices, on_device(): lax.all_to_all(slot_grads.astype(jnp.bfloat16), 'pool', split_axis=0, con...  45.4 us
    and x1, other arithmetic, on_device(): jnp.take(arrived.reshape(owners * capacity, feat_dim), slot_of, axis=0)  35.6 us
    reduce_scatter x1, waiting for transfers between devices, on_device(): lax.psum_scatter((logit_scale * lax.dot_general(grad_coef, query_vec, (((...  32.2 us
    all_gather x1, waiting for transfers between devices, on_device(): blocks = lax.all_gather(item_vec, 'blk', axis=0, tiled=True)  31 us
    all_to_all x1, blocking collectives, on_device(): lax.all_to_all(fetch_rows, 'pool', split_axis=0, concat_axis=0, tiled=True)  22.3 us
    dot_general x1, matrix products, on_device(): lax.dot_general(pre_grad, w_in, (((1,), (1,)), ((), ())), preferred_eleme...  12 us
    scatter-add x1, other arithmetic, on_device(): jax.ops.segment_sum(returned.reshape(owners * capacity, feat_dim), asked_...  11.1 us
    all_to_all x1, starting transfers between devices, on_device(): lax.all_to_all(slot_grads.astype(jnp.bfloat16), 'pool', split_axis=0, con...  10.8 us
  transfers between devices with their start and end apart: 4, of which 4 were waited for; matrix products, arithmetic and copies ran while one was open for 16% of the time, Pallas kernels for 0%

commit v1 on v0

v1 whole, which is shorter than its diff:
```python
import jax
import jax.numpy as jnp
from jax import lax
from jax.sharding import PartitionSpec as P

logit_scale = 80.0
norm_eps = 1e-06


def on_device(query_emb, item_table, w_in, bias_in, w_out, fetch_rows, fetch_counts, pos_slot):
    owners = lax.axis_size("pool")
    blks = lax.axis_size("blk")
    capacity = fetch_rows.shape[1]
    slots = owners * capacity
    pool_rows = item_table.shape[0]
    queries = query_emb.shape[0]
    own = lax.axis_index("blk")

    query_f = query_emb.astype(jnp.float32)
    query_inv = lax.rsqrt(jnp.sum(query_f * query_f, axis=1, keepdims=True) + norm_eps)
    query_vec = (query_f * query_inv).astype(jnp.bfloat16)
    group_vec = lax.all_gather(query_vec, "blk", axis=0, tiled=True)

    asked = lax.all_to_all(fetch_rows, "pool", split_axis=0, concat_axis=0, tiled=True)
    pre_act = jnp.dot(item_table, w_in, preferred_element_type=jnp.float32) + bias_in
    hidden = jax.nn.silu(pre_act).astype(jnp.bfloat16)
    tower_out = jnp.dot(hidden, w_out, preferred_element_type=jnp.float32)
    item_inv = lax.rsqrt(jnp.sum(tower_out * tower_out, axis=1, keepdims=True) + norm_eps)
    item_vec = (tower_out * item_inv).astype(jnp.bfloat16)

    pick = (asked.reshape(slots, 1) == jnp.arange(pool_rows, dtype=jnp.int32)[None, :]).astype(jnp.bfloat16)
    served = jnp.dot(pick, item_vec, preferred_element_type=jnp.float32).astype(jnp.bfloat16)
    arrived = lax.all_to_all(
        served.reshape(owners, capacity, -1), "pool", split_axis=0, concat_axis=0, tiled=True
    ).reshape(slots, -1)

    counts = fetch_counts[0]
    ends = jnp.cumsum(counts)
    slot_column = jnp.arange(capacity, dtype=jnp.int32)
    live = (slot_column[None, :] < counts[:, None]).reshape(slots, 1)
    past = (ends[:, None] <= pos_slot[None, :]).astype(jnp.int32)
    target = jnp.sum(past * (capacity - counts[:, None]), axis=0) + pos_slot
    target = jnp.where(
        (jnp.arange(blks, dtype=jnp.int32) == own)[:, None], target[None, :], -1
    ).reshape(-1)
    hit = jnp.arange(slots, dtype=jnp.int32)[:, None] == target[None, :]

    scores = logit_scale * lax.dot_general(
        arrived, group_vec, (((1,), (1,)), ((), ())), preferred_element_type=jnp.float32
    )
    sums = jnp.sum(jnp.where(live, jnp.exp(scores), 0.0), axis=0)
    picked = jnp.sum(jnp.where(hit, scores, 0.0), axis=0)
    parts = [sums]
    for shift in range(1, blks):
        perm = [(i, (i + shift) % blks) for i in range(blks)]
        parts.append(lax.ppermute(sums, "blk", perm))
    totals = jnp.log(sum(parts[1:], parts[0]))
    mine = lax.dynamic_slice(totals - picked, (own * queries,), (queries,))
    coef = (
        jnp.where(live, jnp.exp(scores - totals[None, :]), 0.0) - hit.astype(jnp.float32)
    ).astype(jnp.bfloat16)
    item_grad = (
        logit_scale * jnp.dot(coef, group_vec, preferred_element_type=jnp.float32)
    ).astype(jnp.bfloat16)
    returned = lax.all_to_all(
        item_grad.reshape(owners, capacity, -1), "pool", split_axis=0, concat_axis=0, tiled=True
    ).reshape(slots, -1)

    part_grad = logit_scale * lax.dot_general(
        coef, arrived, (((0,), (0,)), ((), ())), preferred_element_type=jnp.float32
    )
    vec_grad = lax.psum_scatter(
        part_grad.astype(jnp.bfloat16), "blk", scatter_dimension=0, tiled=True
    ).astype(jnp.float32)
    query_grad = vec_grad * query_inv - query_f * query_inv**3 * jnp.sum(
        query_f * vec_grad, axis=1, keepdims=True
    )

    row_grad = lax.dot_general(
        pick, returned, (((0,), (0,)), ((), ())), preferred_element_type=jnp.float32
    )
    tower_grad = (
        row_grad * item_inv
        - tower_out * item_inv**3 * jnp.sum(tower_out * row_grad, axis=1, keepdims=True)
    ).astype(jnp.bfloat16)
    hidden_grad = lax.dot_general(
        tower_grad, w_out, (((1,), (1,)), ((), ())), preferred_element_type=jnp.float32
    )
    gate_sig = jax.nn.sigmoid(pre_act)
    pre_grad = (hidden_grad * gate_sig * (1.0 + pre_act * (1.0 - gate_sig))).astype(jnp.bfloat16)
    table_grad = lax.dot_general(
        pre_grad, w_in, (((1,), (1,)), ((), ())), preferred_element_type=jnp.float32
    )
    return (mine, query_grad, table_grad)


def solution(mesh):
    placed = (
        P(("pool", "blk"), None),
        P(("pool", "blk"), None),
        P(),
        P(),
        P(),
        P(("pool", "blk"), None),
        P(("pool", "blk"), None),
        P(("pool", "blk")),
    )
    return jax.shard_map(
        on_device,
        mesh=mesh,
        in_specs=placed,
        out_specs=(P(("pool", "blk")), P(("pool", "blk"), None), P(("pool", "blk"), None)),
        check_vma=False,
    )
```

time: 296 us -> 156 us (0.53)
  waiting for transfers between devices: 115 us -> 53.1 us
  other arithmetic: 63.3 us -> 5.19 us
  local copies, waits for them, and re-layouts: 31.9 us -> 3.01 us
  starting transfers between devices: 16.8 us -> 39.6 us
  blocking collectives: 22.3 us -> 0 us
  matrix products: 31.2 us -> 40.1 us
    and x3 -> x0, other arithmetic: 35.7 us -> none  [the longest x1 35.6 us: on_device(): jnp.take(arrived.reshape(owners * capacity, feat_dim), slot_of, axis=0)]
    reduce_scatter x1, waiting for transfers between devices: 32.2 us -> 0.01 us  [on_device(): lax.psum_scatter(part_grad.astype(jnp.bfloat16), 'blk', scatter_dimension...]
    all_to_all x2 -> x3, waiting for transfers between devices: 51.4 us -> 21.9 us  [the longest x1 21.9 us: on_device(): lax.all_to_all(item_grad.reshape(owners, capacity, -1), 'pool', split_axi...]
    gather x8 -> x0, local copies, waits for them, and re-layouts: 26.7 us -> none  [the longest x1 7.43 us: on_device(): jnp.take(padded, inverse, axis=0).reshape(owners, capacity, feat_dim)]
    all_to_all x1 -> x0, blocking collectives: 22.3 us -> none  [on_device(): lax.all_to_all(fetch_rows, 'pool', split_axis=0, concat_axis=0, tiled=True)]
    all_to_all x2 -> x3, starting transfers between devices: 16.5 us -> 36.7 us  [the longest x1 13.2 us: on_device(): lax.all_to_all(item_grad.reshape(owners, capacity, -1), 'pool', split_axi...]
    scatter-add x1 -> x0, other arithmetic: 11.1 us -> none  [on_device(): jax.ops.segment_sum(returned.reshape(owners * capacity, feat_dim), asked_...]
    dot_general x4 -> x6, matrix products: 16.7 us -> 24.1 us  [the longest x1 5.8 us: on_device(): jnp.dot(item_table, w_in, preferred_element_type=jnp.float32) + bias_in]
  transfers between devices with their start and end apart: 4 -> 8, of which waited for: 4 -> 4; matrix products, arithmetic and copies ran while one was open for 16% -> 21% of each run, Pallas kernels for 0% -> 0%
where the time goes in v1:
time: 156 us; the launch traced here: 155 us
  waiting for transfers between devices  53.1 us (34%)
  matrix products  40.1 us (26%)
  starting transfers between devices  39.6 us (25%)
  between operations  14.2 us (9%)
  other arithmetic  5.19 us (3%)
  local copies, waits for them, and re-layouts  3.01 us (2%)
    all_gather x1, waiting for transfers between devices, on_device(): group_vec = lax.all_gather(query_vec, 'blk', axis=0, tiled=True)  28.2 us
    all_to_all x1, waiting for transfers between devices, on_device(): lax.all_to_all(item_grad.reshape(owners, capacity, -1), 'pool', split_axi...  21.9 us
    all_to_all x1, starting transfers between devices, on_device(): lax.all_to_all(item_grad.reshape(owners, capacity, -1), 'pool', split_axi...  13.2 us
    all_to_all x1, starting transfers between devices, on_device(): lax.all_to_all(fetch_rows, 'pool', split_axis=0, concat_axis=0, tiled=True)  13 us
    dot_general x1, matrix products, on_device(): lax.dot_general(pre_grad, w_in, (((1,), (1,)), ((), ())), preferred_eleme...  12.5 us
    all_to_all x1, starting transfers between devices, on_device(): lax.all_to_all(served.reshape(owners, capacity, -1), 'pool', split_axis=0...  10.5 us
    dot_general x1, matrix products, on_device(): jnp.dot(item_table, w_in, preferred_element_type=jnp.float32) + bias_in  5.8 us
    dot_general x1, matrix products, on_device(): lax.dot_general(coef, arrived, (((0,), (0,)), ((), ())), preferred_elemen...  5.33 us
  transfers between devices with their start and end apart: 8, of which 4 were waited for; matrix products, arithmetic and copies ran while one was open for 21% of the time, Pallas kernels for 0%

profile of v1, /device:TPU:1, one launch (start us, length us, event | category | flops | bytes accessed | tf_op | source)
XLA Modules:
  0.0 155.1 jit_solution(15306238734862338263)
XLA Ops:
  7.2 0.0 copy-start
  7.2 1.5 copy.16
  8.7 13.0 %all-to-all-start = ((s32[64,1,16]{2,1,0:T(1,128)}), s32[64,1,16]{2,1,0:T(1,128)S(1)}, u32[]{:S(2)}, u32[]{:S(2)}) async-start(s32[64,1,16]{2,1,0:T(1,128)} %bitcast.1), calls=%async_computation | async-start | bytes 65536 | tf_op jit(solution)/shard_map/all_to_all | solution.py:24
  21.7 0.0 copy-start.5
  21.7 5.8 %fusion.22 = f32[512,3072]{1,0:T(8,128)S(1)} fusion(bf16[512,1024]{1,0:T(8,128)(2,1)} %param.9, bf16[1024,3072]{1,0:T(8,128)(2,1)} %param.10), kind=kOutput, calls=%fused_computation.48 | convolution fusion | flops 3221225472 | bytes 13631488 | tf_op jit(solution)/shard_map/dot_general | solution.py:25
  27.5 0.0 copy-done
  27.5 0.0 copy-done.5
  27.6 0.0 copy-start.6
  27.6 3.5 %multiply_reduce_fusion.1 = (f32[512]{0:T(512)S(1)}, f32[512,512]{0,1:T(8,128)}) fusion(bf16[3072,512]{1,0:T(8,128)(2,1)S(1)} %copy-done, f32[512,3072]{1,0:T(8,128)S(1)} %fusion.22, f32[3072]{0:T(1024)S(1)} %copy-done.5), kind=kOutput, calls=%fused_computation.18 | convolution fusion | flops 1620573696 | bytes 10500096 | tf_op jit(solution)/shard_map/dot_general | solution.py:27
  31.1 0.0 all-to-all-done
  31.1 0.5 broadcast.63
  31.6 0.7 reduce.4
  32.3 0.1 eq.38
  32.4 3.0 %fusion.4 = bf16[1024,512]{1,0:T(8,128)(2,1)} fusion(s32[1024]{0:T(1024)S(1)} %eq.38, f32[512,512]{0,1:T(8,128)} %get-tuple-element.12, f32[512]{0:T(512)S(1)} %get-tuple-element.8), kind=kOutput, calls=%fused_computation.14 | convolution fusion | flops 538443776 | bytes 2103296 | tf_op jit(solution)/shard_map/dot_general | solution.py:32
  35.4 10.5 %all-to-all-start.1 = ((bf16[64,16,512]{2,1,0:T(8,128)(2,1)}), bf16[64,16,512]{2,1,0:T(8,128)(2,1)}, u32[]{:S(2)}, u32[]{:S(2)}) async-start(bf16[64,16,512]{2,1,0:T(8,128)(2,1)} %bitcast.21), calls=%async_computation.1 | async-start | bytes 2097152 | tf_op jit(solution)/shard_map/all_to_all | solution.py:33
  45.9 0.0 all-gather.2.cloned.1.call-start
  45.9 0.1 fusion.8
  46.1 0.8 fusion.9
  46.9 0.0 all-gather.2.cloned.1.call-update
  46.9 0.0 copy-done.3
  46.9 0.1 iota_compare_fusion.6
  47.0 0.1 lt.29
  47.1 0.1 copy.17
  47.2 0.1 reduce-window.8
  47.3 0.1 reduce.1
  47.4 0.1 select_reduce_fusion.2
  47.5 0.1 select_bitcast_fusion
  47.6 28.2 %all-gather.2.cloned.1.call-done = bf16[1024,512]{1,0:T(8,128)(2,1)} async-done(((bf16[256,512]{1,0:T(8,128)(2,1)}), bf16[1024,512]{1,0:T(8,128)(2,1)}) %all-gather.2.cloned.1.call-update) | async-done | bytes 1048592 | tf_op jit(solution)/shard_map/all_gather | solution.py:22
  75.9 0.0 all-to-all-done.1
  75.9 3.7 %select_reduce_fusion = (f32[1024]{0:T(1024)S(1)}, f32[1024]{0:T(1024)S(1)}, f32[1024,1024]{1,0:T(8,128)S(1)}) fusion(s32[1024]{0:T(1024)S(1)} %bitcast.23, pred[1024]{0:T(1024)(128)(4,1)S(1)} %lt.29, bf16[1024,512]{1,0:T(8,128)(2,1)} %bitcast.3, bf16[1024,512]{1,0:T(8,128)(2,1)} %all-gather.2.cloned.1.call-done), kind=kOutput, calls=%fused_computation.4 | convolution fusion | flops 1080031232 | bytes 6304768 | tf_op jit(solution)/shard_map/dot_general | solution.py:48
  79.5 1.3 collective-permute-start.2
  80.8 0.7 collective-permute-start.1
  81.5 0.8 collective-permute-start
  82.3 0.0 collective-permute-done.2
  82.3 2.5 %collective-permute-done.1 = f32[1024]{0:T(1024)S(1)} collective-permute-done((f32[1024]{0:T(1024)S(1)}, f32[1024]{0:T(1024)S(1)}, u32[]{:S(2)}, u32[]{:S(2)}) %collective-permute-start.1) | collective-permute-done | bytes 4128 | tf_op jit(solution)/shard_map/ppermute | solution.py:56
  84.8 0.4 collective-permute-done
  85.2 0.0 copy-done.4
  85.2 2.8 %multiply_convert_fusion.3 = bf16[1024,512]{1,0:T(8,128)(2,1)} fusion(bf16[1024,512]{1,0:T(8,128)(2,1)S(1)} %copy-done.4, f32[1024,1024]{1,0:T(8,128)S(1)} %get-tuple-element.13, f32[1024]{0:T(1024)S(1)} %get-tuple-element.6, s32[1024]{0:T(1024)S(1)} %bitcast.24, pred[1024]{0:T(1024)(128)(4,1)S(1)} %lt.29), kind=kOutput, calls=%fused_computation.9 | convolution fusion | flops 1082130432 | bytes 6300672 | tf_op jit(solution)/shard_map/dot_general | solution.py:63
  88.0 13.2 %all-to-all-start.2 = ((bf16[64,16,512]{2,1,0:T(8,128)(2,1)}), bf16[64,16,512]{2,1,0:T(8,128)(2,1)}, u32[]{:S(2)}, u32[]{:S(2)}) async-start(bf16[64,16,512]{2,1,0:T(8,128)(2,1)} %bitcast.22), calls=%async_computation.3 | async-start | bytes 2097152 | tf_op jit(solution)/shard_map/all_to_all | solution.py:65
  101.3 0.0 reduce-scatter.2.cloned.1.call-start
  101.3 5.3 %multiply_convert_fusion.4 = bf16[1024,512]{1,0:T(8,128)(2,1)} fusion(bf16[1024,512]{1,0:T(8,128)(2,1)} %bitcast.3, f32[1024,1024]{1,0:T(8,128)} %copy-done.7, f32[1024]{0:T(1024)S(1)} %get-tuple-element.6, s32[1024]{0:T(1024)S(1)} %bitcast.25, pred[1024]{0:T(1024)(128)(4,1)S(1)} %lt.29), kind=kOutput, calls=%fused_computation.10 | convolution fusion | flops 1082130432 | bytes 6300672 | tf_op jit(solution)/shard_map/dot_general | solution.py:69
  106.7 0.0 reduce-scatter.2.cloned.1.call-update
  106.7 0.6 dynamic_slice.3
  107.3 21.9 %all-to-all-done.2 = bf16[64,16,512]{2,1,0:T(8,128)(2,1)} async-done(((bf16[64,16,512]{2,1,0:T(8,128)(2,1)}), bf16[64,16,512]{2,1,0:T(8,128)(2,1)}, u32[]{:S(2)}, u32[]{:S(2)}) %all-to-all-start.2) | async-done | bytes 1048608 | tf_op jit(solution)/shard_map/all_to_all | solution.py:65
  129.2 3.6 %multiply_reduce_fusion = (f32[512]{0:T(512)S(1)}, f32[512,512]{0,1:T(8,128)}) fusion(f32[512,512]{0,1:T(8,128)} %get-tuple-element.12, bf16[1024,512]{1,0:T(8,128)(2,1)} %bitcast.6, s32[1024]{0:T(1024)S(1)} %eq.38), kind=kOutput, calls=%fused_computation.16 | convolution fusion | flops 537918976 | bytes 3151872 | tf_op jit(solution)/shard_map/dot_general | solution.py:79
  132.8 12.5 %fusion.1 = f32[512,1024]{1,0:T(8,128)} fusion(bf16[1024,3072]{1,0:T(8,128)(2,1)} %param.10, f32[512,3072]{1,0:T(8,128)} %copy-done.6, bf16[3072,512]{1,0:T(8,128)(2,1)S(1)} %copy-done, f32[3072]{0:T(1024)S(1)} %copy-done.5, f32[512,512]{0,1:T(8,128)} %get-tuple-element.12, f32[512,512]{0,1:T(8,128)} %get-tuple-element.15, f32[512]{0:T(512)S(1)} %get-tuple-element.14, ...), kind=kOutput, calls=%fused_computation.8 | convolution fusion | flops 4848877568 | bytes 19941376 | tf_op jit(solution)/shard_map/dot_general | solution.py:91
  145.2 1.1 fusion.11
  146.3 1.9 %fusion.7 = f32[256,512]{1,0:T(8,128)} fusion(bf16[256,512]{1,0:T(8,128)(2,1)} %reduce-scatter.2.cloned.1.call-done, bf16[256,512]{1,0:T(8,128)(2,1)S(1)} %copy-done.1, f32[256]{0:T(256)S(1)} %fusion.11, f32[256]{0:T(256)S(1)} %get-tuple-element.9, f32[256]{0:T(256)S(1)} %get-tuple-element.10), kind=kLoop, calls=%fused_computation.26 | loop fusion | flops 786432 | bytes 1051648 | tf_op jit(solution)/shard_map/sub | solution.py:75
  (17 shorter events, 0.1 us)
Async XLA Ops:
  7.2 20.4 %copy-start = (bf16[3072,512]{1,0:T(8,128)(2,1)S(1)}, bf16[3072,512]{1,0:T(8,128)(2,1)}, u32[]{:S(2)}) copy-start(bf16[3072,512]{1,0:T(8,128)(2,1)} %param.12) | copy-start | bytes 9437188
  8.7 22.3 %all-to-all-start = ((s32[64,1,16]{2,1,0:T(1,128)}), s32[64,1,16]{2,1,0:T(1,128)S(1)}, u32[]{:S(2)}, u32[]{:S(2)}) async-start(s32[64,1,16]{2,1,0:T(1,128)} %bitcast.1), calls=%async_computation | async-start | bytes 65536 | tf_op jit(solution)/shard_map/all_to_all | solution.py:24
  21.7 5.8 %copy-start.5 = (f32[3072]{0:T(1024)S(1)}, f32[3072]{0:T(1024)}, u32[]{:S(2)}) copy-start(f32[3072]{0:T(1024)} %param.11) | copy-start | bytes 36868
  27.6 3.5 %copy-start.6 = (f32[512,3072]{1,0:T(8,128)}, f32[512,3072]{1,0:T(8,128)S(1)}, u32[]{:S(2)}) copy-start(f32[512,3072]{1,0:T(8,128)S(1)} %fusion.22) | copy-start | bytes 18874372
  31.0 14.9 %copy-start.1 = (bf16[256,512]{1,0:T(8,128)(2,1)S(1)}, bf16[256,512]{1,0:T(8,128)(2,1)}, u32[]{:S(2)}) copy-start(bf16[256,512]{1,0:T(8,128)(2,1)} %param.8) | copy-start | bytes 786436
  31.0 15.9 %copy-start.3 = (s32[1,64]{1,0:T(1,128)S(1)}, s32[1,64]{1,0:T(1,128)}, u32[]{:S(2)}) copy-start(s32[1,64]{1,0:T(1,128)} %param.14) | copy-start | bytes 772
  31.0 16.4 %copy-start.2 = (s32[256]{0:T(256)S(1)}, s32[256]{0:T(256)}, u32[]{:S(2)}) copy-start(s32[256]{0:T(256)} %param.15) | copy-start | bytes 3076
  35.4 40.5 %all-to-all-start.1 = ((bf16[64,16,512]{2,1,0:T(8,128)(2,1)}), bf16[64,16,512]{2,1,0:T(8,128)(2,1)}, u32[]{:S(2)}, u32[]{:S(2)}) async-start(bf16[64,16,512]{2,1,0:T(8,128)(2,1)} %bitcast.21), calls=%async_computation.1 | async-start | bytes 2097152 | tf_op jit(solution)/shard_map/all_to_all | solution.py:33
  45.9 30.0 %all-gather.2.cloned.1.call-start = ((), (), s32[]{:S(2)}) async-start(), calls=%async_computation.4 | async-start | bytes 1310720 | tf_op jit(solution)/shard_map/all_gather | solution.py:22
  75.9 9.4 %copy-start.4 = (bf16[1024,512]{1,0:T(8,128)(2,1)S(1)}, bf16[1024,512]{1,0:T(8,128)(2,1)}, u32[]{:S(2)}) copy-start(bf16[1024,512]{1,0:T(8,128)(2,1)} %all-gather.2.cloned.1.call-done) | copy-start | bytes 3145732
  79.5 8.5 %copy-start.7 = (f32[1024,1024]{1,0:T(8,128)}, f32[1024,1024]{1,0:T(8,128)S(1)}, u32[]{:S(2)}) copy-start(f32[1024,1024]{1,0:T(8,128)S(1)} %get-tuple-element.13) | copy-start | bytes 12582916
  79.5 2.8 %collective-permute-start.2 = (f32[1024]{0:T(1024)S(1)}, f32[1024]{0:T(1024)S(1)}, u32[]{:S(2)}, u32[]{:S(2)}) collective-permute-start(f32[1024]{0:T(1024)S(1)} %get-tuple-element.4), channel_id=1, source_target_pairs={{0,3},{1,0},{2,1},{3,2},{4,7},{5,4},{6,5},{7,6},{8,11},{9,8},{10,9... | collective-permute-start | bytes 12296 | tf_op jit(solution)/shard_map/ppermute | solution.py:56
  80.8 4.0 %collective-permute-start.1 = (f32[1024]{0:T(1024)S(1)}, f32[1024]{0:T(1024)S(1)}, u32[]{:S(2)}, u32[]{:S(2)}) collective-permute-start(f32[1024]{0:T(1024)S(1)} %get-tuple-element.4), channel_id=1, source_target_pairs={{0,2},{1,3},{2,0},{3,1},{4,6},{5,7},{6,4},{7,5},{8,10},{9,11},{10,... | collective-permute-start | bytes 12296 | tf_op jit(solution)/shard_map/ppermute | solution.py:56
  81.5 3.7 %collective-permute-start = (f32[1024]{0:T(1024)S(1)}, f32[1024]{0:T(1024)S(1)}, u32[]{:S(2)}, u32[]{:S(2)}) collective-permute-start(f32[1024]{0:T(1024)S(1)} %get-tuple-element.4), channel_id=1, source_target_pairs={{0,1},{1,2},{2,3},{3,0},{4,5},{5,6},{6,7},{7,4},{8,9},{9,10},{10,1... | collective-permute-start | bytes 12296 | tf_op jit(solution)/shard_map/ppermute | solution.py:56
  88.0 41.1 %all-to-all-start.2 = ((bf16[64,16,512]{2,1,0:T(8,128)(2,1)}), bf16[64,16,512]{2,1,0:T(8,128)(2,1)}, u32[]{:S(2)}, u32[]{:S(2)}) async-start(bf16[64,16,512]{2,1,0:T(8,128)(2,1)} %bitcast.22), calls=%async_computation.3 | async-start | bytes 2097152 | tf_op jit(solution)/shard_map/all_to_all | solution.py:65
  101.3 44.0 %reduce-scatter.2.cloned.1.call-start = ((), (), s32[]{:S(2)}) async-start(), calls=%async_computation.5 | async-start | bytes 1310720 | tf_op jit(solution)/shard_map/reduce_scatter | solution.py:72
Sparse Core Ops, SparseCore 0:
  49.1 26.7 all-gather.1
  106.8 24.0 reduce-scatter.1

commit v2 on v1

v2 whole, which is shorter than its diff:
```python
import functools

import jax
import jax.numpy as jnp
from jax import lax
from jax.experimental import pallas as pl
from jax.experimental.pallas import tpu as pltpu
from jax.sharding import PartitionSpec as P

logit_scale = 80.0
norm_eps = 1e-06
shift = 2.772588722239781

MESH = pl.DeviceIdType.MESH
f32 = jnp.float32
bf16 = jnp.bfloat16
NN = (((1,), (0,)), ((), ()))
NT = (((1,), (1,)), ((), ()))
TN = (((0,), (0,)), ((), ()))


def mm(a, b, dims=NN):
    return lax.dot_general(a, b, dims, preferred_element_type=f32)


def iota(shape, dim):
    return lax.broadcasted_iota(jnp.int32, shape, dim)


def step_kernel(
    n, nb, group,
    query_ref, table_hbm, win_hbm, bias_ref, wout_hbm, rows_ref, counts_ref, pos_ref,
    loss_ref, qgrad_ref, tgrad_hbm,
    table, win, wout, dsilu, tower, item_vec, idx_send, idx_recv, idx_flat, idx_col, idx_row,
    serve, arrive, group_vec, live_col, expo, coef, sums, lossbuf, grad, ret, vg_send, vg_recv,
    row_grad, pre_grad, out_buf,
    w_sem, o_sem, isend, irecv, fsend, frecv, bsend, brecv, qsend, qrecv, ssend, srecv, vsend, vrecv,
):
    p = lax.axis_index("pool")
    b = lax.axis_index("blk")
    cap = rows_ref.shape[1]
    slots = n * cap
    span = group * cap
    groups = n // group
    queries, width = query_ref.shape
    chunks, feats, chunk = win.shape
    pool_rows = table.shape[0]
    outs, out_cols = out_buf.shape[0], out_buf.shape[2]

    def load_table():
        return pltpu.make_async_copy(table_hbm, table, w_sem.at[2 * chunks])

    def load_win(c):
        return pltpu.make_async_copy(
            win_hbm.at[:, pl.ds(pl.multiple_of(c * chunk, chunk), chunk)], win.at[c], w_sem.at[c]
        )

    def load_wout(c):
        return pltpu.make_async_copy(
            wout_hbm.at[pl.ds(pl.multiple_of(c * chunk, chunk), chunk), :],
            wout.at[c],
            w_sem.at[chunks + c],
        )

    def ahead(k):
        return lax.rem(p + k, n)

    def behind(k):
        return lax.rem(p + n - k, n)

    def idx_copy(k):
        return pltpu.make_async_remote_copy(
            src_ref=idx_send.at[k], dst_ref=idx_recv.at[k], send_sem=isend.at[k],
            recv_sem=irecv.at[k], device_id={"pool": ahead(k)}, device_id_type=MESH,
        )

    def rows_of(k):
        return pl.ds(pl.multiple_of(k * cap, cap), cap)

    def fwd_copy(k):
        return pltpu.make_async_remote_copy(
            src_ref=serve.at[rows_of(k)], dst_ref=arrive.at[rows_of(k)], send_sem=fsend.at[k],
            recv_sem=frecv.at[k], device_id={"pool": behind(k)}, device_id_type=MESH,
        )

    def bwd_copy(k):
        return pltpu.make_async_remote_copy(
            src_ref=grad.at[rows_of(k)], dst_ref=ret.at[rows_of(k)], send_sem=bsend.at[k],
            recv_sem=brecv.at[k], device_id={"pool": ahead(k)}, device_id_type=MESH,
        )

    def block_of(c):
        return pl.ds(pl.multiple_of(c * queries, queries), queries)

    def query_copy(j):
        return pltpu.make_async_remote_copy(
            src_ref=group_vec.at[block_of(b)], dst_ref=group_vec.at[block_of(b)],
            send_sem=qsend.at[j], recv_sem=qrecv.at[j],
            device_id={"blk": lax.rem(b + j, nb)}, device_id_type=MESH,
        )

    def query_arrival(j):
        src = lax.rem(b + nb - j, nb)
        return pltpu.make_async_remote_copy(
            src_ref=group_vec.at[block_of(src)], dst_ref=group_vec.at[block_of(src)],
            send_sem=qsend.at[j], recv_sem=qrecv.at[j],
            device_id={"blk": lax.rem(b + j, nb)}, device_id_type=MESH,
        )

    def sums_copy(j):
        return pltpu.make_async_remote_copy(
            src_ref=sums.at[b], dst_ref=sums.at[b], send_sem=ssend.at[j], recv_sem=srecv.at[j],
            device_id={"blk": lax.rem(b + j, nb)}, device_id_type=MESH,
        )

    def sums_arrival(j):
        src = lax.rem(b + nb - j, nb)
        return pltpu.make_async_remote_copy(
            src_ref=sums.at[src], dst_ref=sums.at[src], send_sem=ssend.at[j],
            recv_sem=srecv.at[j],
            device_id={"blk": lax.rem(b + j, nb)}, device_id_type=MESH,
        )

    def vg_copy(j):
        return pltpu.make_async_remote_copy(
            src_ref=vg_send.at[j], dst_ref=vg_recv.at[j], send_sem=vsend.at[j],
            recv_sem=vrecv.at[j],
            device_id={"blk": lax.rem(b + j, nb)}, device_id_type=MESH,
        )

    def loop(low, high, body):
        lax.fori_loop(low, high, lambda k, _: (body(k), 0)[1], 0)

    load_table().start()
    loop(0, chunks, lambda c: (load_win(c).start(), load_wout(c).start()))
    barrier = pltpu.get_barrier_semaphore()

    def greet(k):
        pl.semaphore_signal(barrier, inc=1, device_id={"pool": ahead(k)}, device_id_type=MESH)

    def greet_blk(j):
        pl.semaphore_signal(
            barrier, inc=1, device_id={"blk": lax.rem(b + j, nb)}, device_id_type=MESH
        )

    loop(1, n, greet)
    loop(1, nb, greet_blk)

    query_f = query_ref[...].astype(f32)
    query_inv = lax.rsqrt(jnp.sum(query_f * query_f, axis=1, keepdims=True) + norm_eps)
    group_vec[block_of(b), :] = (query_f * query_inv).astype(bf16)

    idx_send[...] = jnp.zeros_like(idx_send)

    def put_rows(k):
        idx_send[k, :, 0:cap] = rows_ref[pl.ds(ahead(k), 1), :]

    loop(0, n, put_rows)

    counts = counts_ref[...].astype(f32)
    slot_owner = lax.rem(iota((slots, n), 0) // cap + p, n)
    slot_count = jnp.sum(
        jnp.where(slot_owner == iota((slots, n), 1), counts, 0.0), axis=1, keepdims=True
    )
    live_col[...] = (
        lax.rem(iota((slots, 1), 0), cap).astype(f32) < slot_count
    ).astype(f32)
    own_order = iota((n, n), 0)
    other = iota((n, n), 1)
    ends = jnp.sum(jnp.where(other <= own_order, counts, 0.0), axis=1, keepdims=True)
    count_col = jnp.sum(jnp.where(other == own_order, counts, 0.0), axis=1, keepdims=True)
    pos = pos_ref[...].astype(f32)
    past = ends <= pos
    owner = jnp.sum(jnp.where(past, 1.0, 0.0), axis=0, keepdims=True)
    start = jnp.sum(jnp.where(past, count_col, 0.0), axis=0, keepdims=True)
    owner_rel = lax.rem(owner.astype(jnp.int32) + (n - p), n)
    target = owner_rel * cap + (pos - start).astype(jnp.int32)
    target_all = jnp.concatenate([target] * nb, axis=1)
    target_all = jnp.where(iota((1, nb * queries), 1) // queries == b, target_all, -1)

    def tower_chunk(c):
        load_win(c).wait()
        load_wout(c).wait()
        cols = pl.ds(pl.multiple_of(c * chunk, chunk), chunk)
        pre = mm(table[...], win[c]) + bias_ref[:, cols]
        sig = 1.0 / (1.0 + jnp.exp(-pre))
        act = pre * sig
        dsilu[c] = (sig * (1.0 + pre - act)).astype(bf16)
        tower[...] += mm(act.astype(bf16), wout[c])

    tower[...] = jnp.zeros_like(tower)
    load_table().wait()
    early = max(1, chunks // 3)
    loop(0, early, tower_chunk)

    pl.semaphore_wait(barrier, n + nb - 2)
    loop(1, n, lambda k: idx_copy(k).start())
    loop(1, nb, lambda j: query_copy(j).start())
    idx_recv[0] = idx_send[0]
    loop(early, chunks, tower_chunk)

    tower_out = tower[...]
    item_inv = lax.rsqrt(jnp.sum(tower_out * tower_out, axis=1, keepdims=True) + norm_eps)
    item_vec[...] = (tower_out * item_inv).astype(bf16)

    loop(1, n, lambda k: idx_copy(k).wait_recv())

    def flat(k):
        idx_flat[pl.ds(k, 1), :] = idx_recv[k]

    loop(0, n, flat)
    low = lax.rem(idx_flat[...], 16)
    high = (idx_flat[...] - low).astype(f32).astype(bf16)
    low = low.astype(f32).astype(bf16)
    lanes = idx_flat.shape[1]
    spread = (iota((slots, n), 0) // cap == iota((slots, n), 1)).astype(f32).astype(bf16)
    wide = mm(spread, high) + mm(spread, low)
    idx_col[...] = jnp.sum(
        jnp.where(iota((slots, lanes), 1) == lax.rem(iota((slots, lanes), 0), cap), wide, 0.0),
        axis=1, keepdims=True,
    )
    spread_t = (iota((n, slots), 1) // cap == iota((n, slots), 0)).astype(f32).astype(bf16)
    tall = mm(high, spread_t, TN) + mm(low, spread_t, TN)
    idx_row[...] = jnp.sum(
        jnp.where(iota((lanes, slots), 0) == lax.rem(iota((lanes, slots), 1), cap), tall, 0.0),
        axis=0, keepdims=True,
    )

    def span_of(g):
        return pl.ds(pl.multiple_of(g * span, span), span)

    def serve_group(g):
        pick = (
            idx_col[span_of(g), :] == iota((span, pool_rows), 1).astype(f32)
        ).astype(f32).astype(bf16)
        serve[span_of(g), :] = mm(pick, item_vec[...]).astype(bf16)

        def send(i):
            k = g * group + i

            @pl.when(k > 0)
            def _():
                fwd_copy(k).start()

        loop(0, group, send)

    loop(0, groups, serve_group)
    arrive[rows_of(0), :] = serve[rows_of(0), :]

    loop(1, nb, lambda j: query_arrival(j).wait_recv())
    all_queries = nb * queries
    sums[b] = jnp.zeros((1, all_queries), f32)
    lossbuf[...] = jnp.zeros_like(lossbuf)

    def hits(g):
        return iota((span, all_queries), 0) + g * span == target_all

    def score_group(g):
        def arrival(i):
            k = g * group + i

            @pl.when(k > 0)
            def _():
                fwd_copy(k).wait_recv()

        loop(0, group, arrival)
        scores = logit_scale * mm(arrive[span_of(g), :], group_vec[...], NT)
        part = jnp.exp(scores - shift) * live_col[span_of(g), :]
        expo[span_of(g), :] = part
        sums[b] = sums[b] + jnp.sum(part, axis=0, keepdims=True)
        lossbuf[...] += jnp.sum(jnp.where(hits(g), scores, 0.0), axis=0, keepdims=True)

    loop(0, groups, score_group)
    loop(1, nb, lambda j: sums_copy(j).start())
    loop(1, nb, lambda j: sums_arrival(j).wait_recv())
    total = sums[0]
    for j in range(1, nb):
        total = total + sums[j]
    inv_total = 1.0 / total
    lossbuf[...] = jnp.log(total) + shift - lossbuf[...]
    loss_ref[...] = lossbuf[:, block_of(b)]

    def coef_group(g):
        part = expo[span_of(g), :] * inv_total - jnp.where(hits(g), 1.0, 0.0)
        part = part.astype(bf16)
        coef[span_of(g), :] = part
        grad[span_of(g), :] = (logit_scale * mm(part, group_vec[...])).astype(bf16)

        def send(i):
            k = g * group + i

            @pl.when(k > 0)
            def _():
                bwd_copy(k).start()

        loop(0, group, send)

    loop(0, groups, coef_group)
    ret[rows_of(0), :] = grad[rows_of(0), :]

    def part_of(c):
        return logit_scale * mm(coef[:, block_of(c)], arrive[...], TN)

    def send_part(j):
        vg_send[j] = part_of(lax.rem(b + j, nb)).astype(bf16)
        vg_copy(j).start()

    loop(1, nb, send_part)
    vec_grad = part_of(b)

    row_grad[...] = jnp.zeros_like(row_grad)

    def sum_group(g):
        def arrival(i):
            k = g * group + i

            @pl.when(k > 0)
            def _():
                bwd_copy(k).wait_recv()

        loop(0, group, arrival)
        pick_t = (
            iota((pool_rows, span), 0).astype(f32) == idx_row[:, span_of(g)]
        ).astype(f32).astype(bf16)
        row_grad[...] += mm(pick_t, ret[span_of(g), :])

    loop(0, groups // 2, sum_group)
    loop(1, nb, lambda j: vg_copy(j).wait_recv())
    for j in range(1, nb):
        vec_grad = vec_grad + vg_recv[j].astype(f32)
    query_f = query_ref[...].astype(f32)
    qgrad_ref[...] = vec_grad * query_inv - query_f * (query_inv * query_inv * query_inv) * jnp.sum(
        query_f * vec_grad, axis=1, keepdims=True
    )
    loop(groups // 2, groups, sum_group)

    tower_out = tower[...]
    item_inv = lax.rsqrt(jnp.sum(tower_out * tower_out, axis=1, keepdims=True) + norm_eps)
    summed = row_grad[...]
    item_vec[...] = (
        summed * item_inv
        - tower_out * (item_inv * item_inv * item_inv)
        * jnp.sum(tower_out * summed, axis=1, keepdims=True)
    ).astype(bf16)

    def back_chunk(c):
        pre_grad[c] = (mm(item_vec[...], wout[c], NT) * dsilu[c].astype(f32)).astype(bf16)

    loop(0, chunks, back_chunk)

    def out_copy(f):
        return pltpu.make_async_copy(
            out_buf.at[f],
            tgrad_hbm.at[:, pl.ds(pl.multiple_of(f * out_cols, out_cols), out_cols)],
            o_sem.at[f],
        )

    def out_block(f):
        rows = pl.ds(pl.multiple_of(f * out_cols, out_cols), out_cols)
        total = mm(pre_grad[0], win[0, rows, :], NT)
        for c in range(1, chunks):
            total = total + mm(pre_grad[c], win[c, rows, :], NT)
        out_buf[f] = total
        out_copy(f).start()

    loop(0, outs, out_block)

    loop(1, n, lambda k: (idx_copy(k).wait_send(), fwd_copy(k).wait_send(), bwd_copy(k).wait_send()))
    loop(
        1, nb,
        lambda j: (query_copy(j).wait_send(), sums_copy(j).wait_send(), vg_copy(j).wait_send()),
    )
    loop(0, outs, lambda f: out_copy(f).wait())


def on_device(query_emb, item_table, w_in, bias_in, w_out, fetch_rows, fetch_counts, pos_slot):
    n = lax.axis_size("pool")
    nb = lax.axis_size("blk")
    cap = fetch_rows.shape[1]
    slots = n * cap
    queries, width = query_emb.shape
    pool_rows, feats = item_table.shape
    hid = w_in.shape[1]
    chunk = min(512, hid)
    chunks = hid // chunk
    group = min(16, n // 2)
    out_cols = min(256, feats)
    outs = feats // out_cols
    every = nb * queries
    in_vmem = pl.BlockSpec(memory_space=pltpu.VMEM)
    in_any = pl.BlockSpec(memory_space=pl.ANY)
    dma = pltpu.SemaphoreType.DMA
    flops = 2 * pool_rows * hid * (feats + width) * 2 + 6 * slots * every * width
    loss, query_grad, table_grad = pl.pallas_call(
        functools.partial(step_kernel, n, nb, group),
        out_shape=(
            jax.ShapeDtypeStruct((1, queries), f32),
            jax.ShapeDtypeStruct((queries, width), f32),
            jax.ShapeDtypeStruct((pool_rows, feats), f32),
        ),
        in_specs=[in_vmem, in_any, in_any, in_vmem, in_any, in_vmem, in_vmem, in_vmem],
        out_specs=(in_vmem, in_vmem, in_any),
        scratch_shapes=[
            pltpu.VMEM((pool_rows, feats), bf16),
            pltpu.VMEM((chunks, feats, chunk), bf16),
            pltpu.VMEM((chunks, chunk, width), bf16),
            pltpu.VMEM((chunks, pool_rows, chunk), bf16),
            pltpu.VMEM((pool_rows, width), f32),
            pltpu.VMEM((pool_rows, width), bf16),
            pltpu.VMEM((n, 1, 128), jnp.int32),
            pltpu.VMEM((n, 1, 128), jnp.int32),
            pltpu.VMEM((n, 128), jnp.int32),
            pltpu.VMEM((slots, 1), f32),
            pltpu.VMEM((1, slots), f32),
            pltpu.VMEM((slots, width), bf16),
            pltpu.VMEM((slots, width), bf16),
            pltpu.VMEM((every, width), bf16),
            pltpu.VMEM((slots, 1), f32),
            pltpu.VMEM((slots, every), f32),
            pltpu.VMEM((slots, every), bf16),
            pltpu.VMEM((nb, 1, every), f32),
            pltpu.VMEM((1, every), f32),
            pltpu.VMEM((slots, width), bf16),
            pltpu.VMEM((slots, width), bf16),
            pltpu.VMEM((nb, queries, width), bf16),
            pltpu.VMEM((nb, queries, width), bf16),
            pltpu.VMEM((pool_rows, width), f32),
            pltpu.VMEM((chunks, pool_rows, chunk), bf16),
            pltpu.VMEM((outs, pool_rows, out_cols), f32),
            dma((2 * chunks + 1,)),
            dma((outs,)),
            dma((n,)), dma((n,)), dma((n,)), dma((n,)), dma((n,)), dma((n,)),
            dma((nb,)), dma((nb,)), dma((nb,)), dma((nb,)), dma((nb,)), dma((nb,)),
        ],
        compiler_params=pltpu.CompilerParams(
            collective_id=0, has_side_effects=True, vmem_limit_bytes=56 * 1024 * 1024
        ),
        cost_estimate=pl.CostEstimate(
            flops=flops, bytes_accessed=20_000_000, transcendentals=3_000_000
        ),
        name="retrieval_step",
    )(
        query_emb, item_table, w_in, bias_in.reshape(1, hid), w_out, fetch_rows, fetch_counts,
        pos_slot.reshape(1, queries),
    )
    return (loss.reshape(queries), query_grad, table_grad)


def solution(mesh):
    placed = (
        P(("pool", "blk"), None),
        P(("pool", "blk"), None),
        P(),
        P(),
        P(),
        P(("pool", "blk"), None),
        P(("pool", "blk"), None),
        P(("pool", "blk")),
    )
    return jax.shard_map(
        on_device,
        mesh=mesh,
        in_specs=placed,
        out_specs=(P(("pool", "blk")), P(("pool", "blk"), None), P(("pool", "blk"), None)),
        check_vma=False,
    )
```

time: 156 us -> 100 us (0.64)
  Pallas kernels: 0 us -> 91.1 us
  waiting for transfers between devices: 53.1 us -> 0 us
  matrix products: 40.1 us -> 0 us
  starting transfers between devices: 39.6 us -> 0 us
  between operations: 14.2 us -> 0.64 us
  other arithmetic: 5.19 us -> 0 us
  local copies, waits for them, and re-layouts: 3.01 us -> 7.65 us
    pallas_call x0 -> x1, Pallas kernels: none -> 91.1 us  [on_device(): pl.pallas_call(functools.partial(step_kernel, n, nb, group), out_shape=(j...]
    dot_general x8 -> x0, matrix products: 40.1 us -> none  [the longest x1 12.5 us: on_device(): lax.dot_general(pre_grad, w_in, (((1,), (1,)), ((), ())), preferred_eleme...]
    all_to_all x3 -> x0, starting transfers between devices: 36.7 us -> none  [the longest x1 13.2 us: on_device(): lax.all_to_all(item_grad.reshape(owners, capacity, -1), 'pool', split_axi...]
    all_gather x1 -> x0, waiting for transfers between devices: 28.2 us -> none  [on_device(): group_vec = lax.all_gather(query_vec, 'blk', axis=0, tiled=True)]
    all_to_all x3 -> x0, waiting for transfers between devices: 21.9 us -> none  [the longest x1 21.9 us: on_device(): lax.all_to_all(item_grad.reshape(owners, capacity, -1), 'pool', split_axi...]
    unnamed x18 -> x4, local copies, waits for them, and re-layouts: 1.59 us -> 7.65 us
    ppermute x3 -> x0, waiting for transfers between devices: 2.91 us -> none  [on_device(): parts.append(lax.ppermute(sums, 'blk', perm))]
    ppermute x3 -> x0, starting transfers between devices: 2.77 us -> none  [on_device(): parts.append(lax.ppermute(sums, 'blk', perm))]
  transfers between devices with their start and end apart: 8 -> 0, of which waited for: 4 -> 0; matrix products, arithmetic and copies ran while one was open for 21% -> 0% of each run, Pallas kernels for 0% -> 0%
where the time goes in v2:
time: 100 us; the launch traced here: 99.4 us
  Pallas kernels  91.1 us (91%)
  local copies, waits for them, and re-layouts  7.65 us (8%)
    pallas_call x1, Pallas kernels, on_device(): pl.pallas_call(functools.partial(step_kernel, n, nb, group), out_shape=(j...  91.1 us
    unnamed x4, local copies, waits for them, and re-layouts  7.65 us

profile of v2, /device:TPU:1, one launch (start us, length us, event | category | flops | bytes accessed | tf_op | source)
XLA Modules:
  0.0 99.4 jit_solution(8918017378057298858)
XLA Ops:
  0.6 1.4 %copy.11.rows_ref = s32[64,16]{1,0:T(8,128)} copy(s32[64,16]{0,1:T(8,128)} %param.13) | data formatting | bytes 8192 | tf_op args[5]
  2.0 91.1 %retrieval_step.1 = (f32[1,256]{1,0:T(1,128)}, f32[256,512]{1,0:T(8,128)}, f32[512,1024]{1,0:T(8,128)}) custom-call(bf16[256,512]{1,0:T(8,128)(2,1)} %query_ref.1, bf16[512,1024]{1,0:T(8,128)(2,1)} %table_hbm.1, bf16[1024,3072]{1,0:T(8,128)(2,1)} %win_hbm.1, f32[1,3072]{1,0:T(1,128)} %bitcast.4, bf16[3072,512]{1,0:T(8,128)(2,1)} %wout_hbm.1, ...), custom_call_target="tpu_custom_call" | custom-call | flops 12884901888 | bytes 20000000 | tf_op jit(solution)/shard_map/retrieval_step/pallas_call | solution.py:394
  93.1 1.2 %copy.15 = f32[256]{0:T(256)} copy(f32[256]{0:T(256)} %bitcast.3) | data formatting | bytes 2048
  94.4 1.9 %copy.16 = f32[256,512]{1,0:T(8,128)} copy(f32[256,512]{1,0:T(8,128)} %get-tuple-element.13) | data formatting | bytes 1048576
  96.2 3.2 %copy.17 = f32[512,1024]{1,0:T(8,128)} copy(f32[512,1024]{1,0:T(8,128)} %get-tuple-element.14) | data formatting | bytes 4194304

commit v3 on v2

--- a/solution.py
+++ b/solution.py
@@ -9,7 +9,9 @@
 
 logit_scale = 80.0
 norm_eps = 1e-06
-shift = 2.772588722239781
+shift = 4.0
+log2e = 1.4426950408889634
+ln2 = 0.6931471805599453
 
 MESH = pl.DeviceIdType.MESH
 f32 = jnp.float32
@@ -29,16 +31,16 @@
 
 def step_kernel(
     n, nb, group,
-    query_ref, table_hbm, win_hbm, bias_ref, wout_hbm, rows_ref, counts_ref, pos_ref,
-    loss_ref, qgrad_ref, tgrad_hbm,
-    table, win, wout, dsilu, tower, item_vec, idx_send, idx_recv, idx_flat, idx_col, idx_row,
-    serve, arrive, group_vec, live_col, expo, coef, sums, lossbuf, grad, ret, vg_send, vg_recv,
+    query_hbm, table_hbm, win_hbm, bias_hbm, wout_hbm, rows_hbm, counts_hbm, pos_hbm,
+    loss_out, qgrad_out, tgrad_out,
+    query_ref, bias_ref, rows_ref, counts_ref, pos_ref, loss_ref, qgrad_ref, table, win, wout, dsilu, tower, item_vec, idx_send, idx_mid, idx_recv, idx_flat, idx_col, idx_row,
+    serve, arrive, group_vec, live_col, expo, coef, sums, lossbuf, inv_buf, picked, grad, ret, vg_send, vg_recv,
     row_grad, pre_grad, out_buf,
-    w_sem, o_sem, isend, irecv, fsend, frecv, bsend, brecv, qsend, qrecv, ssend, srecv, vsend, vrecv,
+    a_sem, w_sem, o_sem, isend, irecv, fsend, frecv, bsend, brecv, qsend, qrecv, ssend, srecv, vsend, vrecv,
 ):
     p = lax.axis_index("pool")
     b = lax.axis_index("blk")
-    cap = rows_ref.shape[1]
+    cap = rows_ref.shape[0]
     slots = n * cap
     span = group * cap
     groups = n // group
@@ -68,10 +70,41 @@
     def behind(k):
         return lax.rem(p + n - k, n)
 
-    def idx_copy(k):
-        return pltpu.make_async_remote_copy(
-            src_ref=idx_send.at[k], dst_ref=idx_recv.at[k], send_sem=isend.at[k],
-            recv_sem=irecv.at[k], device_id={"pool": ahead(k)}, device_id_type=MESH,
+    plane = idx_send.shape[1]
+    planes = n // plane
+    my_plane = p // plane
+    my_place = lax.rem(p, plane)
+
+    def hop1_copy(k):
+        other = lax.rem(my_plane + k, planes)
+        return pltpu.make_async_remote_copy(
+            src_ref=idx_send.at[other], dst_ref=idx_mid.at[my_plane], send_sem=isend.at[k],
+            recv_sem=irecv.at[k], device_id={"pool": other * plane + my_place},
+            device_id_type=MESH,
+        )
+
+    def hop1_arrival(k):
+        src = lax.rem(my_plane + planes - k, planes)
+        return pltpu.make_async_remote_copy(
+            src_ref=idx_send.at[src], dst_ref=idx_mid.at[src], send_sem=isend.at[k],
+            recv_sem=irecv.at[k], device_id={"pool": src * plane + my_place},
+            device_id_type=MESH,
+        )
+
+    def hop2_copy(k):
+        other = lax.rem(my_place + k, plane)
+        return pltpu.make_async_remote_copy(
+            src_ref=idx_mid.at[:, other], dst_ref=idx_recv.at[my_place],
+            send_sem=isend.at[planes + k], recv_sem=irecv.at[planes + k],
+            device_id={"pool": my_plane * plane + other}, device_id_type=MESH,
+        )
+
+    def hop2_arrival(k):
+        src = lax.rem(my_place + plane - k, plane)
+        return pltpu.make_async_remote_copy(
+            src_ref=idx_mid.at[:, src], dst_ref=idx_recv.at[src],
+            send_sem=isend.at[planes + k], recv_sem=irecv.at[planes + k],
+            device_id={"pool": my_plane * plane + src}, device_id_type=MESH,
         )
 
     def rows_of(k):
@@ -131,6 +164,15 @@
     def loop(low, high, body):
         lax.fori_loop(low, high, lambda k, _: (body(k), 0)[1], 0)
 
+    small = [
+        pltpu.make_async_copy(src, dst, a_sem.at[i])
+        for i, (src, dst) in enumerate((
+            (rows_hbm, rows_ref), (query_hbm, query_ref), (bias_hbm, bias_ref),
+            (counts_hbm, counts_ref), (pos_hbm, pos_ref),
+        ))
+    ]
+    for copy in small:
+        copy.start()
     load_table().start()
     loop(0, chunks, lambda c: (load_win(c).start(), load_wout(c).start()))
     barrier = pltpu.get_barrier_semaphore()
@@ -146,17 +188,105 @@
     loop(1, n, greet)
     loop(1, nb, greet_blk)
 
+    def parts_of(rows):
+        low = lax.rem(rows, 16)
+        return (rows - low).astype(f32).astype(bf16), low.astype(f32).astype(bf16)
+
+    small[0].wait()
+    turn = (iota((n, n), 0) == iota((n, n), 1)).astype(f32).astype(bf16)
+    high, low = parts_of(rows_ref[...])
+    idx_flat[...] = jnp.zeros_like(idx_flat)
+    idx_flat[:, 0:cap] = (mm(turn, high, NT) + mm(turn, low, NT)).astype(jnp.int32)
+
+    def put_rows(k):
+        idx_send[k // plane, lax.rem(k, plane)] = idx_flat[pl.ds(k, 1), :]
+
+    loop(0, n, put_rows)
+
+    def tower_chunk(c):
+        load_win(c).wait()
+        load_wout(c).wait()
+        cols = pl.ds(pl.multiple_of(c * chunk, chunk), chunk)
+        pre = mm(table[...], win[c]) + bias_ref[:, cols]
+        sig = 1.0 / (1.0 + jnp.exp(-pre))
+        act = pre * sig
+        dsilu[c] = (sig * (1.0 + pre - act)).astype(bf16)
+        tower[...] += mm(act.astype(bf16), wout[c])
+
+    small[1].wait()
     query_f = query_ref[...].astype(f32)
     query_inv = lax.rsqrt(jnp.sum(query_f * query_f, axis=1, keepdims=True) + norm_eps)
     group_vec[block_of(b), :] = (query_f * query_inv).astype(bf16)
 
-    idx_send[...] = jnp.zeros_like(idx_send)
-
-    def put_rows(k):
-        idx_send[k, :, 0:cap] = rows_ref[pl.ds(ahead(k), 1), :]
-
-    loop(0, n, put_rows)
-
+    tower[...] = jnp.zeros_like(tower)
+    small[2].wait()
+    load_table().wait()
+    early, middle = max(1, chunks // 3), max(1, chunks // 2)
+    loop(0, early, tower_chunk)
+
+    pl.semaphore_wait(barrier, n + nb - 2)
+    loop(1, planes, lambda k: hop1_copy(k).start())
+    loop(1, nb, lambda j: query_copy(j).start())
+    idx_mid[my_plane] = idx_send[my_plane]
+    loop(early, middle, tower_chunk)
+    loop(1, planes, lambda k: hop1_arrival(k).wait_recv())
+    loop(1, plane, lambda k: hop2_copy(k).start())
+
+    def own_place(z):
+        idx_recv[my_place, z] = idx_mid[z, my_place]
+
+    loop(0, planes, own_place)
+    loop(middle, chunks, tower_chunk)
+
+    tower_out = tower[...]
+    item_inv = lax.rsqrt(jnp.sum(tower_out * tower_out, axis=1, keepdims=True) + norm_eps)
+    item_vec[...] = (tower_out * item_inv).astype(bf16)
+
+    loop(1, plane, lambda k: hop2_arrival(k).wait_recv())
+
+    def flat(k):
+        src = behind(k)
+        idx_flat[pl.ds(k, 1), :] = idx_recv[lax.rem(src, plane), src // plane]
+
+    loop(0, n, flat)
+    high, low = parts_of(idx_flat[...])
+    lanes = idx_flat.shape[1]
+    spread = (iota((slots, n), 0) // cap == iota((slots, n), 1)).astype(f32).astype(bf16)
+    wide = mm(spread, high) + mm(spread, low)
+    idx_col[...] = jnp.sum(
+        jnp.where(iota((slots, lanes), 1) == lax.rem(iota((slots, lanes), 0), cap), wide, 0.0),
+        axis=1, keepdims=True,
+    )
+    spread_t = (iota((n, slots), 1) // cap == iota((n, slots), 0)).astype(f32).astype(bf16)
+    tall = mm(high, spread_t, TN) + mm(low, spread_t, TN)
+    idx_row[...] = jnp.sum(
+        jnp.where(iota((lanes, slots), 0) == lax.rem(iota((lanes, slots), 1), cap), tall, 0.0),
+        axis=0, keepdims=True,
+    )
+
+    def span_of(g):
+        return pl.ds(pl.multiple_of(g * span, span), span)
+
+    def serve_group(g):
+        pick = (
+            idx_col[span_of(g), :] == iota((span, pool_rows), 1).astype(f32)
+        ).astype(f32).astype(bf16)
+        serve[span_of(g), :] = mm(pick, item_vec[...]).astype(bf16)
+
+        def send(i):
+            k = g * group + i
+
+            @pl.when(k > 0)
+            def _():
+                fwd_copy(k).start()
+
+        loop(0, group, send)
+
+    loop(0, groups, serve_group)
+    arrive[rows_of(0), :] = serve[rows_of(0), :]
+
+    small[3].wait()
+    small[4].wait()
     counts = counts_ref[...].astype(f32)
     slot_owner = lax.rem(iota((slots, n), 0) // cap + p, n)
     slot_count = jnp.sum(
@@ -175,85 +305,14 @@
     start = jnp.sum(jnp.where(past, count_col, 0.0), axis=0, keepdims=True)
     owner_rel = lax.rem(owner.astype(jnp.int32) + (n - p), n)
     target = owner_rel * cap + (pos - start).astype(jnp.int32)
-    target_all = jnp.concatenate([target] * nb, axis=1)
-    target_all = jnp.where(iota((1, nb * queries), 1) // queries == b, target_all, -1)
-
-    def tower_chunk(c):
-        load_win(c).wait()
-        load_wout(c).wait()
-        cols = pl.ds(pl.multiple_of(c * chunk, chunk), chunk)
-        pre = mm(table[...], win[c]) + bias_ref[:, cols]
-        sig = 1.0 / (1.0 + jnp.exp(-pre))
-        act = pre * sig
-        dsilu[c] = (sig * (1.0 + pre - act)).astype(bf16)
-        tower[...] += mm(act.astype(bf16), wout[c])
-
-    tower[...] = jnp.zeros_like(tower)
-    load_table().wait()
-    early = max(1, chunks // 3)
-    loop(0, early, tower_chunk)
-
-    pl.semaphore_wait(barrier, n + nb - 2)
-    loop(1, n, lambda k: idx_copy(k).start())
-    loop(1, nb, lambda j: query_copy(j).start())
-    idx_recv[0] = idx_send[0]
-    loop(early, chunks, tower_chunk)
-
-    tower_out = tower[...]
-    item_inv = lax.rsqrt(jnp.sum(tower_out * tower_out, axis=1, keepdims=True) + norm_eps)
-    item_vec[...] = (tower_out * item_inv).astype(bf16)
-
-    loop(1, n, lambda k: idx_copy(k).wait_recv())
-
-    def flat(k):
-        idx_flat[pl.ds(k, 1), :] = idx_recv[k]
-
-    loop(0, n, flat)
-    low = lax.rem(idx_flat[...], 16)
-    high = (idx_flat[...] - low).astype(f32).astype(bf16)
-    low = low.astype(f32).astype(bf16)
-    lanes = idx_flat.shape[1]
-    spread = (iota((slots, n), 0) // cap == iota((slots, n), 1)).astype(f32).astype(bf16)
-    wide = mm(spread, high) + mm(spread, low)
-    idx_col[...] = jnp.sum(
-        jnp.where(iota((slots, lanes), 1) == lax.rem(iota((slots, lanes), 0), cap), wide, 0.0),
-        axis=1, keepdims=True,
-    )
-    spread_t = (iota((n, slots), 1) // cap == iota((n, slots), 0)).astype(f32).astype(bf16)
-    tall = mm(high, spread_t, TN) + mm(low, spread_t, TN)
-    idx_row[...] = jnp.sum(
-        jnp.where(iota((lanes, slots), 0) == lax.rem(iota((lanes, slots), 1), cap), tall, 0.0),
-        axis=0, keepdims=True,
-    )
-
-    def span_of(g):
-        return pl.ds(pl.multiple_of(g * span, span), span)
-
-    def serve_group(g):
-        pick = (
-            idx_col[span_of(g), :] == iota((span, pool_rows), 1).astype(f32)
-        ).astype(f32).astype(bf16)
-        serve[span_of(g), :] = mm(pick, item_vec[...]).astype(bf16)
-
-        def send(i):
-            k = g * group + i
-
-            @pl.when(k > 0)
-            def _():
-                fwd_copy(k).start()
-
-        loop(0, group, send)
-
-    loop(0, groups, serve_group)
-    arrive[rows_of(0), :] = serve[rows_of(0), :]
 
     loop(1, nb, lambda j: query_arrival(j).wait_recv())
     all_queries = nb * queries
     sums[b] = jnp.zeros((1, all_queries), f32)
-    lossbuf[...] = jnp.zeros_like(lossbuf)
+    picked[...] = jnp.zeros_like(picked)
 
     def hits(g):
-        return iota((span, all_queries), 0) + g * span == target_all
+        return iota((span, queries), 0) + g * span == target
 
     def score_group(g):
         def arrival(i):
@@ -264,11 +323,13 @@
                 fwd_copy(k).wait_recv()
 
         loop(0, group, arrival)
-        scores = logit_scale * mm(arrive[span_of(g), :], group_vec[...], NT)
-        part = jnp.exp(scores - shift) * live_col[span_of(g), :]
+        vecs = arrive[span_of(g), :]
+        scores = mm(vecs, group_vec[...], NT)
+        part = jnp.exp2(scores * (logit_scale * log2e) - shift) * live_col[span_of(g), :]
         expo[span_of(g), :] = part
         sums[b] = sums[b] + jnp.sum(part, axis=0, keepdims=True)
-        lossbuf[...] += jnp.sum(jnp.where(hits(g), scores, 0.0), axis=0, keepdims=True)
+        own = mm(vecs, group_vec[block_of(b), :], NT)
+        picked[...] += jnp.sum(jnp.where(hits(g), own, 0.0), axis=0, keepdims=True)
 
     loop(0, groups, score_group)
     loop(1, nb, lambda j: sums_copy(j).start())
@@ -277,14 +338,18 @@
     for j in range(1, nb):
         total = total + sums[j]
     inv_total = 1.0 / total
-    lossbuf[...] = jnp.log(total) + shift - lossbuf[...]
-    loss_ref[...] = lossbuf[:, block_of(b)]
+    inv_buf[...] = inv_total
+    lossbuf[...] = jnp.log(total) + shift * ln2
+    loss_ref[...] = lossbuf[:, block_of(b)] - logit_scale * picked[...]
+    loss_copy = pltpu.make_async_copy(loss_ref, loss_out, o_sem.at[outs])
+    loss_copy.start()
 
     def coef_group(g):
-        part = expo[span_of(g), :] * inv_total - jnp.where(hits(g), 1.0, 0.0)
-        part = part.astype(bf16)
-        coef[span_of(g), :] = part
-        grad[span_of(g), :] = (logit_scale * mm(part, group_vec[...])).astype(bf16)
+        coef[span_of(g), :] = (expo[span_of(g), :] * inv_total).astype(bf16)
+        coef[span_of(g), block_of(b)] = (
+            expo[span_of(g), block_of(b)] * inv_buf[:, block_of(b)] - jnp.where(hits(g), 1.0, 0.0)
+        ).astype(bf16)
+        grad[span_of(g), :] = (logit_scale * mm(coef[span_of(g), :], group_vec[...])).astype(bf16)
 
         def send(i):
             k = g * group + i
@@ -332,6 +397,8 @@
     qgrad_ref[...] = vec_grad * query_inv - query_f * (query_inv * query_inv * query_inv) * jnp.sum(
         query_f * vec_grad, axis=1, keepdims=True
     )
+    qgrad_copy = pltpu.make_async_copy(qgrad_ref, qgrad_out, o_sem.at[outs + 1])
+    qgrad_copy.start()
     loop(groups // 2, groups, sum_group)
 
     tower_out = tower[...]
@@ -351,7 +418,7 @@
     def out_copy(f):
         return pltpu.make_async_copy(
             out_buf.at[f],
-            tgrad_hbm.at[:, pl.ds(pl.multiple_of(f * out_cols, out_cols), out_cols)],
+            tgrad_out.at[:, pl.ds(pl.multiple_of(f * out_cols, out_cols), out_cols)],
             o_sem.at[f],
         )
 
@@ -365,12 +432,43 @@
 
     loop(0, outs, out_block)
 
-    loop(1, n, lambda k: (idx_copy(k).wait_send(), fwd_copy(k).wait_send(), bwd_copy(k).wait_send()))
+    loop(1, planes, lambda k: hop1_copy(k).wait_send())
+    loop(1, plane, lambda k: hop2_copy(k).wait_send())
+    loop(1, n, lambda k: (fwd_copy(k).wait_send(), bwd_copy(k).wait_send()))
     loop(
         1, nb,
         lambda j: (query_copy(j).wait_send(), sums_copy(j).wait_send(), vg_copy(j).wait_send()),
     )
+    loss_copy.wait()
+    qgrad_copy.wait()
     loop(0, outs, lambda f: out_copy(f).wait())
+
+
+def copy_kernel(
+    loss_in, qgrad_in, tgrad_in, loss_out, qgrad_out, tgrad_out, loss_ref, qgrad_ref, tgrad_ref,
+    in_sem, out_sem
+):
+    parts = out_sem.shape[0] - 2
+    rows = tgrad_ref.shape[0] // parts
+    moves = [
+        (tgrad_in.at[pl.ds(i * rows, rows)], tgrad_ref.at[pl.ds(i * rows, rows)],
+         tgrad_out.at[pl.ds(i * rows, rows)])
+        for i in range(parts)
+    ]
+    moves += [(qgrad_in, qgrad_ref, qgrad_out), (loss_in, loss_ref, loss_out)]
+    loads = [
+        pltpu.make_async_copy(src, mid, in_sem.at[i]) for i, (src, mid, _) in enumerate(moves)
+    ]
+    saves = [
+        pltpu.make_async_copy(mid, dst, out_sem.at[i]) for i, (_, mid, dst) in enumerate(moves)
+    ]
+    for load in loads:
+        load.start()
+    for load, save in zip(loads, saves):
+        load.wait()
+        save.start()
+    for save in saves:
+        save.wait()
 
 
 def on_device(query_emb, item_table, w_in, bias_in, w_out, fetch_rows, fetch_counts, pos_slot):
@@ -384,11 +482,11 @@
     chunk = min(512, hid)
     chunks = hid // chunk
     group = min(16, n // 2)
+    plane = 8 if n % 8 == 0 and n > 8 else 2
     out_cols = min(256, feats)
     outs = feats // out_cols
     every = nb * queries
-    in_vmem = pl.BlockSpec(memory_space=pltpu.VMEM)
-    in_any = pl.BlockSpec(memory_space=pl.ANY)
+    in_hbm = pl.BlockSpec(memory_space=pltpu.HBM)
     dma = pltpu.SemaphoreType.DMA
     flops = 2 * pool_rows * hid * (feats + width) * 2 + 6 * slots * every * width
     loss, query_grad, table_grad = pl.pallas_call(
@@ -398,17 +496,25 @@
             jax.ShapeDtypeStruct((queries, width), f32),
             jax.ShapeDtypeStruct((pool_rows, feats), f32),
         ),
-        in_specs=[in_vmem, in_any, in_any, in_vmem, in_any, in_vmem, in_vmem, in_vmem],
-        out_specs=(in_vmem, in_vmem, in_any),
+        in_specs=[in_hbm] * 8,
+        out_specs=(in_hbm, in_hbm, in_hbm),
         scratch_shapes=[
+            pltpu.VMEM((queries, width), bf16),
+            pltpu.VMEM((1, hid), f32),
+            pltpu.VMEM((cap, n), jnp.int32),
+            pltpu.VMEM((1, n), jnp.int32),
+            pltpu.VMEM((1, queries), jnp.int32),
+            pltpu.VMEM((1, queries), f32),
+            pltpu.VMEM((queries, width), f32),
             pltpu.VMEM((pool_rows, feats), bf16),
             pltpu.VMEM((chunks, feats, chunk), bf16),
             pltpu.VMEM((chunks, chunk, width), bf16),
             pltpu.VMEM((chunks, pool_rows, chunk), bf16),
             pltpu.VMEM((pool_rows, width), f32),
             pltpu.VMEM((pool_rows, width), bf16),
-            pltpu.VMEM((n, 1, 128), jnp.int32),
-            pltpu.VMEM((n, 1, 128), jnp.int32),
+            pltpu.VMEM((n // plane, plane, 1, 128), jnp.int32),
+            pltpu.VMEM((n // plane, plane, 1, 128), jnp.int32),
+            pltpu.VMEM((plane, n // plane, 1, 128), jnp.int32),
             pltpu.VMEM((n, 128), jnp.int32),
             pltpu.VMEM((slots, 1), f32),
             pltpu.VMEM((1, slots), f32),
@@ -420,6 +526,8 @@
             pltpu.VMEM((slots, every), bf16),
             pltpu.VMEM((nb, 1, every), f32),
             pltpu.VMEM((1, every), f32),
+            pltpu.VMEM((1, every), f32),
+            pltpu.VMEM((1, queries), f32),
             pltpu.VMEM((slots, width), bf16),
             pltpu.VMEM((slots, width), bf16),
             pltpu.VMEM((nb, queries, width), bf16),
@@ -427,22 +535,45 @@
             pltpu.VMEM((pool_rows, width), f32),
             pltpu.VMEM((chunks, pool_rows, chunk), bf16),
             pltpu.VMEM((outs, pool_rows, out_cols), f32),
+            dma((5,)),
             dma((2 * chunks + 1,)),
-            dma((outs,)),
-            dma((n,)), dma((n,)), dma((n,)), dma((n,)), dma((n,)), dma((n,)),
+            dma((outs + 2,)),
+            dma((plane + n // plane,)), dma((plane + n // plane,)),
+            dma((n,)), dma((n,)), dma((n,)), dma((n,)),
             dma((nb,)), dma((nb,)), dma((nb,)), dma((nb,)), dma((nb,)), dma((nb,)),
         ],
         compiler_params=pltpu.CompilerParams(
-            collective_id=0, has_side_effects=True, vmem_limit_bytes=56 * 1024 * 1024
+            collective_id=0, has_side_effects=True, vmem_limit_bytes=60 * 1024 * 1024
         ),
         cost_estimate=pl.CostEstimate(
             flops=flops, bytes_accessed=20_000_000, transcendentals=3_000_000
         ),
         name="retrieval_step",
     )(
-        query_emb, item_table, w_in, bias_in.reshape(1, hid), w_out, fetch_rows, fetch_counts,
+        query_emb, item_table, w_in, bias_in.reshape(1, hid), w_out, fetch_rows.T, fetch_counts,
         pos_slot.reshape(1, queries),
     )
+    parts = 4
+    loss, query_grad, table_grad = pl.pallas_call(
+        copy_kernel,
+        out_shape=(
+            jax.ShapeDtypeStruct((1, queries), f32),
+            jax.ShapeDtypeStruct((queries, width), f32),
+            jax.ShapeDtypeStruct((pool_rows, feats), f32),
+        ),
+        in_specs=[in_hbm] * 3,
+        out_specs=(in_hbm, in_hbm, in_hbm),
+        scratch_shapes=[
+            pltpu.VMEM((1, queries), f32),
+            pltpu.VMEM((queries, width), f32),
+            pltpu.VMEM((pool_rows, feats), f32),
+            dma((parts + 2,)),
+            dma((parts + 2,)),
+        ],
+        compiler_params=pltpu.CompilerParams(vmem_limit_bytes=60 * 1024 * 1024),
+        cost_estimate=pl.CostEstimate(flops=0, bytes_accessed=6_000_000, transcendentals=0),
+        name="results",
+    )(loss, query_grad, table_grad)
     return (loss.reshape(queries), query_grad, table_grad)
 
 

time: 100 us -> 95.1 us (0.951)
  local copies, waits for them, and re-layouts: 7.65 us -> 0 us
  Pallas kernels: 91.1 us -> 93.5 us
    unnamed x4 -> x0, local copies, waits for them, and re-layouts: 7.65 us -> none
    pallas_call x0 -> x1, Pallas kernels: none -> 2.63 us  [on_device(): pl.pallas_call(copy_kernel, out_shape=(jax.ShapeDtypeStruct((1, queries),...]
where the time goes in v3:
time: 95.1 us; the launch traced here: 94.2 us
  Pallas kernels  93.5 us (98%)
    pallas_call x1, Pallas kernels, on_device(): pl.pallas_call(functools.partial(step_kernel, n, nb, group), out_shape=(j...  90.9 us
    pallas_call x1, Pallas kernels, on_device(): pl.pallas_call(copy_kernel, out_shape=(jax.ShapeDtypeStruct((1, queries),...  2.63 us

profile of v3, /device:TPU:1, one launch (start us, length us, event | category | flops | bytes accessed | tf_op | source)
XLA Modules:
  0.0 94.2 jit_solution(14026307141632663926)
XLA Ops:
  0.6 90.9 %retrieval_step.1 = (f32[1,256]{1,0:T(1,128)}, f32[256,512]{1,0:T(8,128)}, f32[512,1024]{1,0:T(8,128)}) custom-call(bf16[256,512]{1,0:T(8,128)(2,1)} %query_hbm.1, bf16[512,1024]{1,0:T(8,128)(2,1)} %table_hbm.1, bf16[1024,3072]{1,0:T(8,128)(2,1)} %win_hbm.1, f32[1,3072]{1,0:T(1,128)} %bitcast.4, bf16[3072,512]{1,0:T(8,128)(2,1)} %wout_hbm.1, ...), custom_call_target="tpu_custom_call" | custom-call | flops 12884901888 | bytes 20000000 | tf_op jit(solution)/shard_map/retrieval_step/pallas_call | solution.py:492
  91.5 2.6 %results.1 = (f32[1,256]{1,0:T(1,128)}, f32[256,512]{1,0:T(8,128)}, f32[512,1024]{1,0:T(8,128)}) custom-call(f32[1,256]{1,0:T(1,128)} %get-tuple-element.9.loss_in, f32[256,512]{1,0:T(8,128)} %get-tuple-element.10.qgrad_in, f32[512,1024]{1,0:T(8,128)} %get-tuple-element.11.tgrad_in), custom_call_target="tpu_custom_call" | custom-call | bytes 6000000 | tf_op jit(solution)/shard_map/results/pallas_call | solution.py:557

commit v4 on v3

--- a/solution.py
+++ b/solution.py
@@ -70,41 +70,46 @@
     def behind(k):
         return lax.rem(p + n - k, n)
 
-    plane = idx_send.shape[1]
-    planes = n // plane
+    planes, plane = idx_recv.shape[0], idx_recv.shape[1]
     my_plane = p // plane
     my_place = lax.rem(p, plane)
 
+    def place_at(k):
+        return lax.rem(my_place + k, plane)
+
+    def plane_at(k):
+        return lax.rem(my_plane + k, planes)
+
     def hop1_copy(k):
-        other = lax.rem(my_plane + k, planes)
-        return pltpu.make_async_remote_copy(
-            src_ref=idx_send.at[other], dst_ref=idx_mid.at[my_plane], send_sem=isend.at[k],
-            recv_sem=irecv.at[k], device_id={"pool": other * plane + my_place},
+        other = place_at(k)
+        return pltpu.make_async_remote_copy(
+            src_ref=idx_send.at[other], dst_ref=idx_mid.at[my_place], send_sem=isend.at[k],
+            recv_sem=irecv.at[k], device_id={"pool": my_plane * plane + other},
             device_id_type=MESH,
         )
 
     def hop1_arrival(k):
-        src = lax.rem(my_plane + planes - k, planes)
+        src = place_at(plane - k)
         return pltpu.make_async_remote_copy(
             src_ref=idx_send.at[src], dst_ref=idx_mid.at[src], send_sem=isend.at[k],
-            recv_sem=irecv.at[k], device_id={"pool": src * plane + my_place},
+            recv_sem=irecv.at[k], device_id={"pool": my_plane * plane + src},
             device_id_type=MESH,
         )
 
     def hop2_copy(k):
-        other = lax.rem(my_place + k, plane)
-        return pltpu.make_async_remote_copy(
-            src_ref=idx_mid.at[:, other], dst_ref=idx_recv.at[my_place],
-            send_sem=isend.at[planes + k], recv_sem=irecv.at[planes + k],
-            device_id={"pool": my_plane * plane + other}, device_id_type=MESH,
+        other = plane_at(k)
+        return pltpu.make_async_remote_copy(
+            src_ref=idx_mid.at[:, other], dst_ref=idx_recv.at[my_plane],
+            send_sem=isend.at[plane + k], recv_sem=irecv.at[plane + k],
+            device_id={"pool": other * plane + my_place}, device_id_type=MESH,
         )
 
     def hop2_arrival(k):
-        src = lax.rem(my_place + plane - k, plane)
+        src = plane_at(planes - k)
         return pltpu.make_async_remote_copy(
             src_ref=idx_mid.at[:, src], dst_ref=idx_recv.at[src],
-            send_sem=isend.at[planes + k], recv_sem=irecv.at[planes + k],
-            device_id={"pool": my_plane * plane + src}, device_id_type=MESH,
+            send_sem=isend.at[plane + k], recv_sem=irecv.at[plane + k],
+            device_id={"pool": src * plane + my_place}, device_id_type=MESH,
         )
 
     def rows_of(k):
@@ -163,6 +168,15 @@
 
     def loop(low, high, body):
         lax.fori_loop(low, high, lambda k, _: (body(k), 0)[1], 0)
+
+    barrier = pltpu.get_barrier_semaphore()
+
+    def greet(device):
+        pl.semaphore_signal(barrier, inc=1, device_id=device, device_id_type=MESH)
+
+    loop(1, plane, lambda k: greet({"pool": my_plane * plane + place_at(k)}))
+    loop(1, planes, lambda k: greet({"pool": plane_at(k) * plane + my_place}))
+    loop(1, nb, lambda j: greet({"blk": lax.rem(b + j, nb)}))
 
     small = [
         pltpu.make_async_copy(src, dst, a_sem.at[i])
@@ -175,18 +189,6 @@
         copy.start()
     load_table().start()
     loop(0, chunks, lambda c: (load_win(c).start(), load_wout(c).start()))
-    barrier = pltpu.get_barrier_semaphore()
-
-    def greet(k):
-        pl.semaphore_signal(barrier, inc=1, device_id={"pool": ahead(k)}, device_id_type=MESH)
-
-    def greet_blk(j):
-        pl.semaphore_signal(
-            barrier, inc=1, device_id={"blk": lax.rem(b + j, nb)}, device_id_type=MESH
-        )
-
-    loop(1, n, greet)
-    loop(1, nb, greet_blk)
 
     def parts_of(rows):
         low = lax.rem(rows, 16)
@@ -199,7 +201,7 @@
     idx_flat[:, 0:cap] = (mm(turn, high, NT) + mm(turn, low, NT)).astype(jnp.int32)
 
     def put_rows(k):
-        idx_send[k // plane, lax.rem(k, plane)] = idx_flat[pl.ds(k, 1), :]
+        idx_send[lax.rem(k, plane), k // plane] = idx_flat[pl.ds(k, 1), :]
 
     loop(0, n, put_rows)
 
@@ -207,11 +209,15 @@
         load_win(c).wait()
         load_wout(c).wait()
         cols = pl.ds(pl.multiple_of(c * chunk, chunk), chunk)
-        pre = mm(table[...], win[c]) + bias_ref[:, cols]
-        sig = 1.0 / (1.0 + jnp.exp(-pre))
-        act = pre * sig
-        dsilu[c] = (sig * (1.0 + pre - act)).astype(bf16)
-        tower[...] += mm(act.astype(bf16), wout[c])
+        half = 0.5 * (mm(table[...], win[c]) + bias_ref[:, cols])
+        tanh = jnp.tanh(half)
+        bent = half * tanh
+        tower[...] += mm((half + bent).astype(bf16), wout[c])
+        dsilu[c] = ((0.5 + 0.5 * tanh) * (1.0 + (half - bent))).astype(bf16)
+
+    pl.semaphore_wait(barrier, plane + planes + nb - 3)
+    loop(1, plane, lambda k: hop1_copy(k).start())
+    idx_mid[my_place] = idx_send[my_place]
 
     small[1].wait()
     query_f = query_ref[...].astype(f32)
@@ -221,32 +227,25 @@
     tower[...] = jnp.zeros_like(tower)
     small[2].wait()
     load_table().wait()
-    early, middle = max(1, chunks // 3), max(1, chunks // 2)
-    loop(0, early, tower_chunk)
-
-    pl.semaphore_wait(barrier, n + nb - 2)
-    loop(1, planes, lambda k: hop1_copy(k).start())
-    loop(1, nb, lambda j: query_copy(j).start())
-    idx_mid[my_plane] = idx_send[my_plane]
-    loop(early, middle, tower_chunk)
-    loop(1, planes, lambda k: hop1_arrival(k).wait_recv())
-    loop(1, plane, lambda k: hop2_copy(k).start())
-
-    def own_place(z):
-        idx_recv[my_place, z] = idx_mid[z, my_place]
-
-    loop(0, planes, own_place)
-    loop(middle, chunks, tower_chunk)
+    loop(0, 1, tower_chunk)
+    loop(1, plane, lambda k: hop1_arrival(k).wait_recv())
+    loop(1, planes, lambda k: hop2_copy(k).start())
+
+    def own_plane(r):
+        idx_recv[my_plane, r] = idx_mid[r, my_plane]
+
+    loop(0, plane, own_plane)
+    loop(1, chunks, tower_chunk)
 
     tower_out = tower[...]
     item_inv = lax.rsqrt(jnp.sum(tower_out * tower_out, axis=1, keepdims=True) + norm_eps)
     item_vec[...] = (tower_out * item_inv).astype(bf16)
 
-    loop(1, plane, lambda k: hop2_arrival(k).wait_recv())
+    loop(1, planes, lambda k: hop2_arrival(k).wait_recv())
 
     def flat(k):
         src = behind(k)
-        idx_flat[pl.ds(k, 1), :] = idx_recv[lax.rem(src, plane), src // plane]
+        idx_flat[pl.ds(k, 1), :] = idx_recv[src // plane, lax.rem(src, plane)]
 
     loop(0, n, flat)
     high, low = parts_of(idx_flat[...])
@@ -257,6 +256,30 @@
         jnp.where(iota((slots, lanes), 1) == lax.rem(iota((slots, lanes), 0), cap), wide, 0.0),
         axis=1, keepdims=True,
     )
+    def span_of(g):
+        return pl.ds(pl.multiple_of(g * span, span), span)
+
+    def serve_group(g):
+        pick = (
+            idx_col[span_of(g), :] == iota((span, pool_rows), 1).astype(f32)
+        ).astype(f32).astype(bf16)
+        serve[span_of(g), :] = mm(pick, item_vec[...]).astype(bf16)
+
+        def send(i):
+            k = g * group + i
+
+            @pl.when(k > 0)
+            def _():
+                fwd_copy(k).start()
+
+        loop(0, group, send)
+
+        @pl.when(g < nb - 1)
+        def _():
+            query_copy(g + 1).start()
+
+    loop(0, groups, serve_group)
+    arrive[rows_of(0), :] = serve[rows_of(0), :]
     spread_t = (iota((n, slots), 1) // cap == iota((n, slots), 0)).astype(f32).astype(bf16)
     tall = mm(high, spread_t, TN) + mm(low, spread_t, TN)
     idx_row[...] = jnp.sum(
@@ -264,26 +287,6 @@
         axis=0, keepdims=True,
     )
 
-    def span_of(g):
-        return pl.ds(pl.multiple_of(g * span, span), span)
-
-    def serve_group(g):
-        pick = (
-            idx_col[span_of(g), :] == iota((span, pool_rows), 1).astype(f32)
-        ).astype(f32).astype(bf16)
-        serve[span_of(g), :] = mm(pick, item_vec[...]).astype(bf16)
-
-        def send(i):
-            k = g * group + i
-
-            @pl.when(k > 0)
-            def _():
-                fwd_copy(k).start()
-
-        loop(0, group, send)
-
-    loop(0, groups, serve_group)
-    arrive[rows_of(0), :] = serve[rows_of(0), :]
 
     small[3].wait()
     small[4].wait()
@@ -413,7 +416,7 @@
     def back_chunk(c):
         pre_grad[c] = (mm(item_vec[...], wout[c], NT) * dsilu[c].astype(f32)).astype(bf16)
 
-    loop(0, chunks, back_chunk)
+    loop(0, chunks // 2, lambda i: (back_chunk(2 * i), back_chunk(2 * i + 1)))
 
     def out_copy(f):
         return pltpu.make_async_copy(
@@ -430,10 +433,13 @@
         out_buf[f] = total
         out_copy(f).start()
 
-    loop(0, outs, out_block)
-
-    loop(1, planes, lambda k: hop1_copy(k).wait_send())
-    loop(1, plane, lambda k: hop2_copy(k).wait_send())
+    if outs % 2:
+        loop(0, outs, out_block)
+    else:
+        loop(0, outs // 2, lambda i: (out_block(2 * i), out_block(2 * i + 1)))
+
+    loop(1, plane, lambda k: hop1_copy(k).wait_send())
+    loop(1, planes, lambda k: hop2_copy(k).wait_send())
     loop(1, n, lambda k: (fwd_copy(k).wait_send(), bwd_copy(k).wait_send()))
     loop(
         1, nb,
@@ -512,9 +518,9 @@
             pltpu.VMEM((chunks, pool_rows, chunk), bf16),
             pltpu.VMEM((pool_rows, width), f32),
             pltpu.VMEM((pool_rows, width), bf16),
+            pltpu.VMEM((plane, n // plane, 1, 128), jnp.int32),
+            pltpu.VMEM((plane, n // plane, 1, 128), jnp.int32),
             pltpu.VMEM((n // plane, plane, 1, 128), jnp.int32),
-            pltpu.VMEM((n // plane, plane, 1, 128), jnp.int32),
-            pltpu.VMEM((plane, n // plane, 1, 128), jnp.int32),
             pltpu.VMEM((n, 128), jnp.int32),
             pltpu.VMEM((slots, 1), f32),
             pltpu.VMEM((1, slots), f32),

time: 95.1 us -> 94 us (0.988)
  Pallas kernels: 93.5 us -> 91.7 us
    pallas_call x1, Pallas kernels: 90.9 us -> 89.1 us  [on_device(): pl.pallas_call(functools.partial(step_kernel, n, nb, group), out_shape=(j...]
where the time goes in v4:
time: 94 us; the launch traced here: 92.4 us
  Pallas kernels  91.7 us (98%)
    pallas_call x1, Pallas kernels, on_device(): pl.pallas_call(functools.partial(step_kernel, n, nb, group), out_shape=(j...  89.1 us
    pallas_call x1, Pallas kernels, on_device(): pl.pallas_call(copy_kernel, out_shape=(jax.ShapeDtypeStruct((1, queries),...  2.63 us

profile of v4, /device:TPU:1, one launch (start us, length us, event | category | flops | bytes accessed | tf_op | source)
XLA Modules:
  0.0 92.4 jit_solution(2663556099249038819)
XLA Ops:
  0.6 89.1 %retrieval_step.1 = (f32[1,256]{1,0:T(1,128)}, f32[256,512]{1,0:T(8,128)}, f32[512,1024]{1,0:T(8,128)}) custom-call(bf16[256,512]{1,0:T(8,128)(2,1)} %query_hbm.1, bf16[512,1024]{1,0:T(8,128)(2,1)} %table_hbm.1, bf16[1024,3072]{1,0:T(8,128)(2,1)} %win_hbm.1, f32[1,3072]{1,0:T(1,128)} %bitcast.4, bf16[3072,512]{1,0:T(8,128)(2,1)} %wout_hbm.1, ...), custom_call_target="tpu_custom_call" | custom-call | flops 12884901888 | bytes 20000000 | tf_op jit(solution)/shard_map/retrieval_step/pallas_call | solution.py:498
  89.7 2.6 %results.1 = (f32[1,256]{1,0:T(1,128)}, f32[256,512]{1,0:T(8,128)}, f32[512,1024]{1,0:T(8,128)}) custom-call(f32[1,256]{1,0:T(1,128)} %get-tuple-element.9.loss_in, f32[256,512]{1,0:T(8,128)} %get-tuple-element.10.qgrad_in, f32[512,1024]{1,0:T(8,128)} %get-tuple-element.11.tgrad_in), custom_call_target="tpu_custom_call" | custom-call | bytes 6000000 | tf_op jit(solution)/shard_map/results/pallas_call | solution.py:563

commit v5 on v4

--- a/solution.py
+++ b/solution.py
@@ -278,7 +278,7 @@
         def _():
             query_copy(g + 1).start()
 
-    loop(0, groups, serve_group)
+    loop(0, groups, lambda g: serve_group(lax.rem(g + 1, groups)))
     arrive[rows_of(0), :] = serve[rows_of(0), :]
     spread_t = (iota((n, slots), 1) // cap == iota((n, slots), 0)).astype(f32).astype(bf16)
     tall = mm(high, spread_t, TN) + mm(low, spread_t, TN)
@@ -334,7 +334,7 @@
         own = mm(vecs, group_vec[block_of(b), :], NT)
         picked[...] += jnp.sum(jnp.where(hits(g), own, 0.0), axis=0, keepdims=True)
 
-    loop(0, groups, score_group)
+    loop(0, groups, lambda g: score_group(lax.rem(g * 3, groups)))
     loop(1, nb, lambda j: sums_copy(j).start())
     loop(1, nb, lambda j: sums_arrival(j).wait_recv())
     total = sums[0]
@@ -363,7 +363,7 @@
 
         loop(0, group, send)
 
-    loop(0, groups, coef_group)
+    loop(0, groups, lambda g: coef_group(lax.rem(g + 1, groups)))
     ret[rows_of(0), :] = grad[rows_of(0), :]
 
     def part_of(c):
@@ -375,6 +375,10 @@
 
     loop(1, nb, send_part)
     vec_grad = part_of(b)
+    loop(1, plane, lambda k: hop1_copy(k).wait_send())
+    loop(1, planes, lambda k: hop2_copy(k).wait_send())
+    loop(1, n, lambda k: fwd_copy(k).wait_send())
+    loop(1, nb, lambda j: (query_copy(j).wait_send(), sums_copy(j).wait_send()))
 
     row_grad[...] = jnp.zeros_like(row_grad)
 
@@ -392,7 +396,7 @@
         ).astype(f32).astype(bf16)
         row_grad[...] += mm(pick_t, ret[span_of(g), :])
 
-    loop(0, groups // 2, sum_group)
+    loop(0, groups // 2, lambda g: sum_group(lax.rem(g * 3, groups)))
     loop(1, nb, lambda j: vg_copy(j).wait_recv())
     for j in range(1, nb):
         vec_grad = vec_grad + vg_recv[j].astype(f32)
@@ -402,7 +406,7 @@
     )
     qgrad_copy = pltpu.make_async_copy(qgrad_ref, qgrad_out, o_sem.at[outs + 1])
     qgrad_copy.start()
-    loop(groups // 2, groups, sum_group)
+    loop(groups // 2, groups, lambda g: sum_group(lax.rem(g * 3, groups)))
 
     tower_out = tower[...]
     item_inv = lax.rsqrt(jnp.sum(tower_out * tower_out, axis=1, keepdims=True) + norm_eps)
@@ -416,7 +420,7 @@
     def back_chunk(c):
         pre_grad[c] = (mm(item_vec[...], wout[c], NT) * dsilu[c].astype(f32)).astype(bf16)
 
-    loop(0, chunks // 2, lambda i: (back_chunk(2 * i), back_chunk(2 * i + 1)))
+    loop(0, chunks, back_chunk)
 
     def out_copy(f):
         return pltpu.make_async_copy(
@@ -438,13 +442,8 @@
     else:
         loop(0, outs // 2, lambda i: (out_block(2 * i), out_block(2 * i + 1)))
 
-    loop(1, plane, lambda k: hop1_copy(k).wait_send())
-    loop(1, planes, lambda k: hop2_copy(k).wait_send())
-    loop(1, n, lambda k: (fwd_copy(k).wait_send(), bwd_copy(k).wait_send()))
-    loop(
-        1, nb,
-        lambda j: (query_copy(j).wait_send(), sums_copy(j).wait_send(), vg_copy(j).wait_send()),
-    )
+    loop(1, n, lambda k: bwd_copy(k).wait_send())
+    loop(1, nb, lambda j: vg_copy(j).wait_send())
     loss_copy.wait()
     qgrad_copy.wait()
     loop(0, outs, lambda f: out_copy(f).wait())
@@ -485,7 +484,7 @@
     queries, width = query_emb.shape
     pool_rows, feats = item_table.shape
     hid = w_in.shape[1]
-    chunk = min(512, hid)
+    chunk = min(1024, hid)
     chunks = hid // chunk
     group = min(16, n // 2)
     plane = 8 if n % 8 == 0 and n > 8 else 2

time: 94 us -> 92 us (0.979); the launches traced: 92.4 us -> 91.9 us
  no operation moved by 1% of the time
where the time goes in v5:
time: 92 us; the launch traced here: 91.9 us
  Pallas kernels  91.2 us (99%)
    pallas_call x1, Pallas kernels, on_device(): pl.pallas_call(functools.partial(step_kernel, n, nb, group), out_shape=(j...  88.6 us
    pallas_call x1, Pallas kernels, on_device(): pl.pallas_call(copy_kernel, out_shape=(jax.ShapeDtypeStruct((1, queries),...  2.63 us

profile of v5, /device:TPU:1, one launch (start us, length us, event | category | flops | bytes accessed | tf_op | source)
XLA Modules:
  0.0 91.9 jit_solution(2437901671246545258)
XLA Ops:
  0.6 88.6 %retrieval_step.1 = (f32[1,256]{1,0:T(1,128)}, f32[256,512]{1,0:T(8,128)}, f32[512,1024]{1,0:T(8,128)}) custom-call(bf16[256,512]{1,0:T(8,128)(2,1)} %query_hbm.1, bf16[512,1024]{1,0:T(8,128)(2,1)} %table_hbm.1, bf16[1024,3072]{1,0:T(8,128)(2,1)} %win_hbm.1, f32[1,3072]{1,0:T(1,128)} %bitcast.4, bf16[3072,512]{1,0:T(8,128)(2,1)} %wout_hbm.1, ...), custom_call_target="tpu_custom_call" | custom-call | flops 12884901888 | bytes 20000000 | tf_op jit(solution)/shard_map/retrieval_step/pallas_call | solution.py:497
  89.3 2.6 %results.1 = (f32[1,256]{1,0:T(1,128)}, f32[256,512]{1,0:T(8,128)}, f32[512,1024]{1,0:T(8,128)}) custom-call(f32[1,256]{1,0:T(1,128)} %get-tuple-element.9.loss_in, f32[256,512]{1,0:T(8,128)} %get-tuple-element.10.qgrad_in, f32[512,1024]{1,0:T(8,128)} %get-tuple-element.11.tgrad_in), custom_call_target="tpu_custom_call" | custom-call | bytes 6000000 | tf_op jit(solution)/shard_map/results/pallas_call | solution.py:562

commit v6 on v5

--- a/solution.py
+++ b/solution.py
@@ -34,7 +34,7 @@
     query_hbm, table_hbm, win_hbm, bias_hbm, wout_hbm, rows_hbm, counts_hbm, pos_hbm,
     loss_out, qgrad_out, tgrad_out,
     query_ref, bias_ref, rows_ref, counts_ref, pos_ref, loss_ref, qgrad_ref, table, win, wout, dsilu, tower, item_vec, idx_send, idx_mid, idx_recv, idx_flat, idx_col, idx_row,
-    serve, arrive, group_vec, live_col, expo, coef, sums, lossbuf, inv_buf, picked, grad, ret, vg_send, vg_recv,
+    serve, arrive, group_vec, inv_col, live_col, expo, coef, sums, lossbuf, inv_buf, picked, grad, ret, vg_send, vg_recv,
     row_grad, pre_grad, out_buf,
     a_sem, w_sem, o_sem, isend, irecv, fsend, frecv, bsend, brecv, qsend, qrecv, ssend, srecv, vsend, vrecv,
 ):
@@ -239,6 +239,7 @@
 
     tower_out = tower[...]
     item_inv = lax.rsqrt(jnp.sum(tower_out * tower_out, axis=1, keepdims=True) + norm_eps)
+    inv_col[...] = item_inv
     item_vec[...] = (tower_out * item_inv).astype(bf16)
 
     loop(1, planes, lambda k: hop2_arrival(k).wait_recv())
@@ -375,6 +376,7 @@
 
     loop(1, nb, send_part)
     vec_grad = part_of(b)
+    tower[...] = tower[...] * inv_col[...]
     loop(1, plane, lambda k: hop1_copy(k).wait_send())
     loop(1, planes, lambda k: hop2_copy(k).wait_send())
     loop(1, n, lambda k: fwd_copy(k).wait_send())
@@ -408,13 +410,10 @@
     qgrad_copy.start()
     loop(groups // 2, groups, lambda g: sum_group(lax.rem(g * 3, groups)))
 
-    tower_out = tower[...]
-    item_inv = lax.rsqrt(jnp.sum(tower_out * tower_out, axis=1, keepdims=True) + norm_eps)
     summed = row_grad[...]
+    unit = tower[...]
     item_vec[...] = (
-        summed * item_inv
-        - tower_out * (item_inv * item_inv * item_inv)
-        * jnp.sum(tower_out * summed, axis=1, keepdims=True)
+        inv_col[...] * (summed - unit * jnp.sum(unit * summed, axis=1, keepdims=True))
     ).astype(bf16)
 
     def back_chunk(c):
@@ -526,6 +525,7 @@
             pltpu.VMEM((slots, width), bf16),
             pltpu.VMEM((slots, width), bf16),
             pltpu.VMEM((every, width), bf16),
+            pltpu.VMEM((pool_rows, 1), f32),
             pltpu.VMEM((slots, 1), f32),
             pltpu.VMEM((slots, every), f32),
             pltpu.VMEM((slots, every), bf16),

time: 92 us -> 92 us (level)
  no operation moved by 1% of the time
where the time goes in v6:
time: 92 us; the launch traced here: 91.8 us
  Pallas kernels  91.2 us (99%)
    pallas_call x1, Pallas kernels, on_device(): pl.pallas_call(functools.partial(step_kernel, n, nb, group), out_shape=(j...  88.6 us
    pallas_call x1, Pallas kernels, on_device(): pl.pallas_call(copy_kernel, out_shape=(jax.ShapeDtypeStruct((1, queries),...  2.63 us

profile of v6, /device:TPU:1, one launch (start us, length us, event | category | flops | bytes accessed | tf_op | source)
XLA Modules:
  0.0 91.8 jit_solution(15731218549419425326)
XLA Ops:
  0.6 88.6 %retrieval_step.1 = (f32[1,256]{1,0:T(1,128)}, f32[256,512]{1,0:T(8,128)}, f32[512,1024]{1,0:T(8,128)}) custom-call(bf16[256,512]{1,0:T(8,128)(2,1)} %query_hbm.1, bf16[512,1024]{1,0:T(8,128)(2,1)} %table_hbm.1, bf16[1024,3072]{1,0:T(8,128)(2,1)} %win_hbm.1, f32[1,3072]{1,0:T(1,128)} %bitcast.4, bf16[3072,512]{1,0:T(8,128)(2,1)} %wout_hbm.1, ...), custom_call_target="tpu_custom_call" | custom-call | flops 12884901888 | bytes 20000000 | tf_op jit(solution)/shard_map/retrieval_step/pallas_call | solution.py:496
  89.2 2.6 %results.1 = (f32[1,256]{1,0:T(1,128)}, f32[256,512]{1,0:T(8,128)}, f32[512,1024]{1,0:T(8,128)}) custom-call(f32[1,256]{1,0:T(1,128)} %get-tuple-element.9.loss_in, f32[256,512]{1,0:T(8,128)} %get-tuple-element.10.qgrad_in, f32[512,1024]{1,0:T(8,128)} %get-tuple-element.11.tgrad_in), custom_call_target="tpu_custom_call" | custom-call | bytes 6000000 | tf_op jit(solution)/shard_map/results/pallas_call | solution.py:562
